TPU v7x, 256 devices: a whole 4x4x8 slice. The times are simulated.
256 devices in a mesh: dp: 8 (over x, core), graph: 32 (over z, y).
Axes of the slice: x: 4, y: 4, z: 8, core: 2. Of those that a mesh axis runs over, the one named last changes fastest.
Arguments:
- node_feats: bfloat16 [8, 512, 3712], P('dp', 'graph'), may hold values from -6 to 6
- node_cotan: bfloat16 [8, 512, 3712], P('dp', 'graph'), may hold values from -6 to 6
- source: int32 [8, 10240], P('dp', 'graph'), may hold values from 0 to 511, as said below
- target: int32 [8, 10240], P('dp', 'graph'), may hold values from 0 to 511, as said below
- angle: float32 [8, 10240], P('dp', 'graph'), may hold values from -3.140625 to 3.140625
- w_zero: bfloat16 [896, 896], replicated, may hold values from -0.1875 to 0.1875
- w_one: bfloat16 [768, 1536], replicated, may hold values from -0.21875 to 0.21875
- w_two: bfloat16 [640, 1280], replicated, may hold values from -0.25 to 0.25
Outputs:
- grad_nodes: bfloat16 [8, 512, 3712], P('dp', 'graph')
- grad_zero: float32 [896, 896], P('graph')
- grad_one: float32 [768, 1536], P('graph')
- grad_two: float32 [640, 1280], P('graph')
Inputs may be any that keep to these rules, and one draw needn't show every extreme that they name: `source`: the edges at positions d * 320 to (d + 1) * 320 - 1 of a batch have both ends among atoms d * 16 - 8 to (d + 1) * 16 + 7; the first and the last of these atoms that lie in the batch are named on every device; no edge joins an atom to itself. `target`: as for source, with the same ranges per device.
All inputs are finite; a program needn't handle non-finite values.
Results may differ from a plain program's by a relative error of at most 0.0015.
The roundings to bfloat16 on the way count: a program that leaves them out, or rounds other values in their place, can miss the bound.
Values may be sent and summed in bfloat16 or wider, within the bound.
A program may use at most 128 MiB of HBM per device.

v0:
```python
import jax
import jax.numpy as jnp
from jax import lax
from jax.sharding import Mesh
from jax.sharding import PartitionSpec as P

HEADS = 8
GRAPH = ("graph_0", "graph_1")


def padded_2(cells, sides, width):
    for axis, dim in sides:
        count = lax.axis_size(axis)
        ends = count - 1
        head = lax.slice_in_dim(cells, 0, width, axis=dim)
        tail = lax.slice_in_dim(cells, cells.shape[dim] - width, cells.shape[dim], axis=dim)
        cells = jnp.concatenate(
            [
                lax.ppermute(tail, axis, [(i, (i + 1) % count) for i in range(ends)]),
                cells,
                lax.ppermute(head, axis, [((i + 1) % count, i) for i in range(ends)]),
            ],
            axis=dim,
        )
    return cells


def shifted(block, axis, distance):
    devices = range(lax.axis_size(axis))
    route = [(i - distance, i) for i in devices if i - distance in devices]
    return lax.ppermute(block, axis, route)


def own_rows_2(running, axes):
    for axis in axes:
        running = lax.psum_scatter(running, axis, scatter_dimension=0, tiled=True)
    return running


def from_everyone(array, axis):
    copies = jnp.broadcast_to(array, (lax.axis_size(axis), *array.shape))
    return lax.all_to_all(copies, axis, split_axis=0, concat_axis=0, tiled=True)


def of_everyone(array, axis):
    everything = from_everyone(array, axis)
    return jnp.sum(everything, axis=0)


def in_one(arrays, axis):
    ends = [0]
    for a in arrays:
        ends.append(ends[-1] + a.size)
    running = of_everyone(jnp.concatenate([a.ravel() for a in arrays]), axis)
    return tuple((running[b:e].reshape(a.shape) for a, b, e in zip(arrays, ends, ends[1:])))


def contract_rows(first, second):
    return lax.dot_general(
        first, second, (((0,), (0,)), ((), ())), preferred_element_type=jnp.float32
    )


def contract_cols(first, weight):
    return lax.dot_general(
        first, weight, (((1,), (1,)), ((), ())), preferred_element_type=jnp.float32
    )


def rotate(first, second, cosine, sine):
    return (cosine * first - sine * second, sine * first + cosine * second)


def per_head(block, channels, heads):
    return block.reshape(block.shape[0], -1, heads, channels // heads)


def edge_terms(feats, cotan, phases, w_zero, w_one, w_two, channels, heads):
    count = feats.shape[0]
    bounds = [0, 7 * channels, 13 * channels, 19 * channels, 24 * channels, 29 * channels]
    cos_one = jnp.cos(phases)[:, None]
    sin_one = jnp.sin(phases)[:, None]
    cos_two = jnp.cos(2.0 * phases)[:, None]
    sin_two = jnp.sin(2.0 * phases)[:, None]
    zero_in = feats[:, : bounds[1]]
    pieces = [feats[:, bounds[k] : bounds[k + 1]].astype(jnp.float32) for k in range(1, 5)]
    rot_p1, rot_n1 = rotate(pieces[0], pieces[1], cos_one, sin_one)
    rot_p2, rot_n2 = rotate(pieces[2], pieces[3], cos_two, sin_two)
    stack_one = jnp.concatenate([rot_p1.astype(jnp.bfloat16), rot_n1.astype(jnp.bfloat16)], 0)
    stack_two = jnp.concatenate([rot_p2.astype(jnp.bfloat16), rot_n2.astype(jnp.bfloat16)], 0)
    zero_out = jnp.dot(zero_in, w_zero, preferred_element_type=jnp.float32)
    prod_one = jnp.dot(stack_one, w_one, preferred_element_type=jnp.float32)
    prod_two = jnp.dot(stack_two, w_two, preferred_element_type=jnp.float32)
    half_one = 6 * channels
    half_two = 5 * channels
    out_p1 = prod_one[:count, :half_one] - prod_one[count:, half_one:]
    out_n1 = prod_one[:count, half_one:] + prod_one[count:, :half_one]
    out_p2 = prod_two[:count, :half_two] - prod_two[count:, half_two:]
    out_n2 = prod_two[:count, half_two:] + prod_two[count:, :half_two]
    scale = 1.0 / jnp.sqrt(jnp.float32(channels // heads))
    logits = per_head(zero_out[:, :channels], channels, heads).sum(axis=(1, 3)) * scale
    gate = jax.nn.sigmoid(logits)
    grads_in = [cotan[:, bounds[k] : bounds[k + 1]].astype(jnp.float32) for k in range(5)]
    du_zero = grads_in[0]
    du_p1, du_n1 = rotate(grads_in[1], grads_in[2], cos_one, sin_one)
    du_p2, du_n2 = rotate(grads_in[3], grads_in[4], cos_two, sin_two)
    dgate = jnp.zeros((count, heads), jnp.float32)
    for upstream, forward in (
        (du_zero, zero_out),
        (du_p1, out_p1),
        (du_n1, out_n1),
        (du_p2, out_p2),
        (du_n2, out_n2),
    ):
        dgate = dgate + per_head(upstream * forward, channels, heads).sum(axis=(1, 3))
    dlogit = dgate * gate * (1.0 - gate) * scale

    def gated(block):
        shaped = per_head(block, channels, heads) * gate[:, None, :, None]
        return shaped.reshape(count, -1)

    dz_zero = gated(du_zero)
    dz_zero = jnp.concatenate(
        [
            dz_zero[:, :channels] + jnp.repeat(dlogit, channels // heads, axis=1),
            dz_zero[:, channels:],
        ],
        1,
    )
    dz_zero = dz_zero.astype(jnp.bfloat16)
    dz_p1, dz_n1, dz_p2, dz_n2 = (gated(du_p1), gated(du_n1), gated(du_p2), gated(du_n2))
    grad_one = jnp.concatenate(
        [jnp.concatenate([dz_p1, dz_n1], 1), jnp.concatenate([dz_n1, -dz_p1], 1)], 0
    ).astype(jnp.bfloat16)
    grad_two = jnp.concatenate(
        [jnp.concatenate([dz_p2, dz_n2], 1), jnp.concatenate([dz_n2, -dz_p2], 1)], 0
    ).astype(jnp.bfloat16)
    back_zero = contract_cols(dz_zero, w_zero)
    back_one = contract_cols(grad_one, w_one)
    back_two = contract_cols(grad_two, w_two)
    dp_one, dn_one = rotate(back_one[:count], back_one[count:], cos_one, -sin_one)
    dp_two, dn_two = rotate(back_two[:count], back_two[count:], cos_two, -sin_two)
    node_terms = jnp.concatenate([back_zero, dp_one, dn_one, dp_two, dn_two], 1)
    return (node_terms, (zero_in, dz_zero), (stack_one, grad_one), (stack_two, grad_two))


def weight_term(operands):
    inputs, upstream = operands
    return contract_rows(inputs, upstream)


def shards(node_feats, node_cotan, source, target, angle, w_zero, w_one, w_two):
    atom_count = node_feats.shape[1]
    row_width = node_feats.shape[2]
    channels = row_width // 29
    position = lax.axis_index(GRAPH)
    reach = atom_count // 2
    stacked = jnp.stack([node_feats[0], node_cotan[0]], 0)
    padded = padded_2(stacked, ((GRAPH, 1),), reach)
    feat_table = padded[0]
    cotan_table = padded[1]
    first_atom = position * atom_count - reach
    src_local = source[0] - first_atom
    dst_local = target[0] - first_atom
    node_terms, pair_zero, pair_one, pair_two = edge_terms(
        feat_table[src_local],
        cotan_table[dst_local],
        angle[0],
        w_zero,
        w_one,
        w_two,
        channels,
        HEADS,
    )
    collected = (
        jnp.zeros((atom_count + 2 * reach, row_width), jnp.float32).at[src_local].add(node_terms)
    )
    from_next = shifted(collected[:reach], GRAPH, -1)
    from_prev = shifted(collected[atom_count + reach :], GRAPH, 1)
    own_rows = collected[reach : reach + atom_count]
    own_rows = own_rows + jnp.pad(from_prev, ((0, atom_count - reach), (0, 0)))
    own_rows = own_rows + jnp.pad(from_next, ((atom_count - reach, 0), (0, 0)))
    grad_nodes = own_rows.astype(jnp.bfloat16)[None]
    part_zero = own_rows_2(weight_term(pair_zero), GRAPH)
    part_one = own_rows_2(weight_term(pair_one), GRAPH)
    part_two = own_rows_2(weight_term(pair_two), GRAPH)
    totals = in_one((part_zero, part_one, part_two), "dp")
    batches = lax.axis_size("dp")
    return (grad_nodes, totals[0] / batches, totals[1] / batches, totals[2] / batches)


def solution(mesh):
    finer = Mesh(mesh.devices.reshape(mesh.shape["dp"], 8, 4), ("dp", "graph_0", "graph_1"))
    placed = (
        P("dp", GRAPH, None),
        P("dp", GRAPH, None),
        P("dp", GRAPH),
        P("dp", GRAPH),
        P("dp", GRAPH),
        P(),
        P(),
        P(),
    )
    return jax.shard_map(
        shards,
        mesh=finer,
        in_specs=placed,
        out_specs=(P("dp", GRAPH, None), P(GRAPH, None), P(GRAPH, None), P(GRAPH, None)),
        check_vma=False,
    )
```

profile of v0, /device:TPU:1, one launch (start us, length us, event | category | flops | bytes accessed | tf_op | source)
XLA Modules:
  0.0 293.6 jit_solution(5334128570818812067)
XLA Ops:
  9.2 4.0 %collective-permute-start = (bf16[2,8,3712]{2,1,0:T(8,128)(2,1)S(1)}, bf16[2,8,3712]{2,1,0:T(8,128)(2,1)S(1)}, u32[]{:S(2)}, u32[]{:S(2)}) collective-permute-start(bf16[2,8,3712]{2,1,0:T(8,128)(2,1)S(1)} %get-tuple-element.36), channel_id=1, source_target_pairs={{0,1},{1,2},{2,3},{3,4},{4,5},{5,6},{6,7},{7,8},{8,9},{9,10},{10,1... | collective-permute-start | bytes 356360 | tf_op jit(solution)/shard_map/ppermute | solution.py:19
  18.9 3.8 %gather_fusion.1 = bf16[320,3712]{1,0:T(8,128)(2,1)} fusion(bf16[32,3712]{1,0:T(8,128)(2,1)S(1)} %get-tuple-element.35, s32[1024]{0:T(1024)S(1)} %pad_clamp_fusion), kind=kCustom, calls=%fused_computation.1 | custom fusion | bytes 4752640 | tf_op jit(solution)/shard_map/gather | solution.py:166
  30.2 3.9 %gather_fusion = bf16[320,3712]{1,0:T(8,128)(2,1)} fusion(bf16[32,3712]{1,0:T(8,128)(2,1)S(1)} %get-tuple-element.34, s32[1024]{0:T(1024)S(1)} %pad_clamp_fusion.1), kind=kCustom, calls=%fused_computation | custom fusion | bytes 4752640 | tf_op jit(solution)/shard_map/gather | solution.py:167
  37.3 3.1 %fusion.47 = (bf16[320,768]{1,0:T(8,128)(2,1)S(1)}, bf16[320,768]{1,0:T(8,128)(2,1)S(1)}, bf16[320,768]{1,0:T(8,128)(2,1)S(1)}, f32[320,768]{1,0:T(8,128)}, f32[320,768]{1,0:T(8,128)}) fusion(f32[320,768]{1,0:T(8,128)S(1)} %copy-done.2, bf16[320,3712]{1,0:T(8,128)(2,1)} %gather_fusion, f32[320]{0:T(512)S(1)} %get-tuple-element.7, ...), kind=kLoop, calls=%fused_computation.109 | loop fusion | flops 4423680 | bytes 9341440 | tf_op jit(solution)/shard_map/convert.10
  41.5 4.2 %fusion.20 = f32[768,1536]{1,0:T(8,128)} fusion(bf16[320,768]{1,0:T(8,128)(2,1)S(1)} %get-tuple-element.27, bf16[320,768]{1,0:T(8,128)(2,1)S(1)} %get-tuple-element.26, bf16[320,768]{1,0:T(8,128)(2,1)S(1)} %get-tuple-element.17, bf16[320,768]{1,0:T(8,128)(2,1)S(1)} %get-tuple-element.18, bf16[320,768]{1,0:T(8,128)(2,1)S(1)} %get-tuple-element.16), kind=kOutput, calls=%fused_computation.57 | convolution fusion | flops 1519779840 | bytes 7176192 | tf_op jit(solution)/shard_map/dot_general | solution.py:59
  50.2 3.0 %convert_multiply_fusion = (f32[320,896]{1,0:T(8,128)}, f32[320,896]{1,0:T(8,128)}) fusion(f32[320,896]{1,0:T(8,128)} %copy-done.5, bf16[320,3712]{1,0:T(8,128)(2,1)} %gather_fusion, f32[320,896]{1,0:T(8,128)S(1)} %copy.49), kind=kLoop, calls=%fused_computation.6 | loop fusion | flops 860160 | bytes 5160960 | tf_op jit(solution)/shard_map/mul | solution.py:115
  53.3 2.8 copy.50
  62.0 3.3 %fusion.46 = (bf16[320,640]{1,0:T(8,128)(2,1)}, bf16[320,640]{1,0:T(8,128)(2,1)}, bf16[320,640]{1,0:T(8,128)(2,1)}, f32[320,640]{1,0:T(8,128)}, f32[320,640]{1,0:T(8,128)}) fusion(f32[320,640]{1,0:T(8,128)S(1)} %copy-done.3, bf16[320,3712]{1,0:T(8,128)(2,1)} %gather_fusion, f32[320]{0:T(512)S(1)} %get-tuple-element.5, f32[320]{0:T(512)S(1)} %get-tuple-element.6, ...), kind=kLoop, calls=%fused_computation.108 | loop fusion | flops 3686400 | bytes 7784960 | tf_op jit(solution)/shard_map/convert.4
  78.1 4.0 %fusion.25 = f32[896,896]{1,0:T(8,128)} fusion(bf16[320,3712]{1,0:T(8,128)(2,1)} %gather_fusion.1, bf16[320,768]{1,0:T(8,128)(2,1)} %slice.268, bf16[320,128]{1,0:T(8,128)(2,1)S(1)} %fusion.34), kind=kOutput, calls=%fused_computation.63 | convolution fusion | flops 514949120 | bytes 4358144 | tf_op jit(solution)/shard_map/dot_general | solution.py:59
  83.2 4.6 %fusion.23 = f32[640,1280]{1,0:T(8,128)} fusion(bf16[320,640]{1,0:T(8,128)(2,1)S(1)} %copy-done.15, bf16[320,640]{1,0:T(8,128)(2,1)S(1)} %copy-done.13, bf16[320,640]{1,0:T(8,128)(2,1)} %get-tuple-element.20, bf16[320,640]{1,0:T(8,128)(2,1)} %get-tuple-element.21, bf16[320,640]{1,0:T(8,128)(2,1)} %get-tuple-element.19), kind=kOutput, calls=%fused_computation.61 | convolution fusion | flops 1056768000 | bytes 5324800 | tf_op jit(solution)/shard_map/dot_general | solution.py:59
  89.8 3.5 %convolution_dynamic-update-slice_fusion = f32[320,3712]{1,0:T(8,128)} fusion(bf16[896,896]{1,0:T(8,128)(2,1)} %param.13, bf16[320,768]{1,0:T(8,128)(2,1)S(1)} %copy-done.4, bf16[320,128]{1,0:T(8,128)(2,1)S(1)} %fusion.34), kind=kOutput, calls=%fused_computation.5 | convolution fusion | flops 514949120 | bytes 3325952 | tf_op jit(solution)/shard_map/dot_general | solution.py:65
  96.0 3.0 %fusion.22 = f32[640,768]{1,0:T(8,128)} fusion(bf16[768,1536]{1,0:T(8,128)(2,1)S(1)} %copy-done, bf16[320,768]{1,0:T(8,128)(2,1)S(1)} %copy-done.9, bf16[320,768]{1,0:T(8,128)(2,1)S(1)} %copy-done.11, bf16[320,768]{1,0:T(8,128)(2,1)S(1)} %copy-done.7), kind=kOutput, calls=%fused_computation.59 | convolution fusion | flops 1517813760 | bytes 5799936 | tf_op jit(solution)/shard_map/dot_general | solution.py:65
  98.9 13.4 %reduce-scatter.11.cloned.1.call-done = f32[96,1536]{1,0:T(8,128)} async-done(((f32[768,1536]{1,0:T(8,128)}), f32[96,1536]{1,0:T(8,128)}) %reduce-scatter.11.cloned.1.call-update) | async-done | bytes 589840 | tf_op jit(solution)/shard_map/reduce_scatter | solution.py:36
  115.1 43.3 %reduce-scatter.9.cloned.1.call-done = f32[112,896]{1,0:T(8,128)} async-done(((f32[896,896]{1,0:T(8,128)}), f32[112,896]{1,0:T(8,128)}) %reduce-scatter.9.cloned.1.call-update) | async-done | bytes 401424 | tf_op jit(solution)/shard_map/reduce_scatter | solution.py:36
  158.3 50.1 %reduce-scatter.15.cloned.1.call-done = f32[80,1280]{1,0:T(8,128)} async-done(((f32[640,1280]{1,0:T(8,128)}), f32[80,1280]{1,0:T(8,128)}) %reduce-scatter.15.cloned.1.call-update) | async-done | bytes 409616 | tf_op jit(solution)/shard_map/reduce_scatter | solution.py:36
  208.4 15.1 %fusion.48 = (f32[24,1280]{1,0:T(8,128)S(1)}, f32[32,896]{1,0:T(8,128)S(1)}) fusion(f32[80,1280]{1,0:T(8,128)} %reduce-scatter.15.cloned.1.call-done, f32[112,896]{1,0:T(8,128)} %reduce-scatter.9.cloned.1.call-done), kind=kCustom, calls=%all-reduce-scatter.2 | all-reduce-scatter fusion | flops 237570 | bytes 1049600
  227.7 3.1 %collective-permute-start.5 = (f32[12,1280]{1,0:T(8,128)S(1)}, f32[12,1280]{1,0:T(8,128)S(1)}, u32[]{:S(2)}, u32[]{:S(2)}) collective-permute-start(f32[12,1280]{1,0:T(8,128)S(1)} %slice.181), channel_id=1, source_target_pairs={{0,1},{1,2},{2,3},{4,5},{5,6},{6,7},{8,9},{9,10},{10,11},{12,13},{... | collective-permute-start | bytes 184328
  235.4 3.0 %broadcast_in_dim.11 = f32[8,1,87552]{2,1,0:T(1,128)} broadcast(f32[87552]{0:T(1024)S(1)} %pad_maximum_fusion.10), dimensions={2} | broadcast | bytes 3151872 | tf_op jit(solution)/shard_map/broadcast_in_dim | solution.py:41
  238.5 8.7 %all-to-all-start = ((f32[8,1,87552]{2,1,0:T(1,128)}), f32[8,1,87552]{2,1,0:T(1,128)}, u32[]{:S(2)}, u32[]{:S(2)}) async-start(f32[8,1,87552]{2,1,0:T(1,128)} %broadcast_in_dim.11), calls=%async_computation.4 | async-start | bytes 5603328 | tf_op jit(solution)/shard_map/all_to_all | solution.py:42
  250.9 8.6 %scatter_custom_fusion = f32[32,3712]{1,0:T(8,128)S(1)} fusion(s32[320]{0:T(512)} %copy-done.25, f32[320,3712]{1,0:T(8,128)} %add_dynamic-update-slice_fusion.1, f32[]{:T(128)} %constant.13.clone.1), kind=kCustom, calls=%fused_computation.75 | custom fusion | flops 1187840 | bytes 475648 | tf_op jit(solution)/shard_map/scatter-add | solution.py:176
  259.5 4.0 %collective-permute-start.2 = (f32[8,3712]{1,0:T(8,128)S(1)}, f32[8,3712]{1,0:T(8,128)S(1)}, u32[]{:S(2)}, u32[]{:S(2)}) collective-permute-start(f32[8,3712]{1,0:T(8,128)S(1)} %get-tuple-element.32), channel_id=1, source_target_pairs={{0,1},{1,2},{2,3},{3,4},{4,5},{5,6},{6,7},{7,8},{8,9},{9,10},{10,1... | collective-permute-start | bytes 356360 | tf_op jit(solution)/shard_map/ppermute | solution.py:31
  266.0 3.9 %collective-permute-done.3 = f32[8,3712]{1,0:T(8,128)S(1)} collective-permute-done((f32[8,3712]{1,0:T(8,128)S(1)}, f32[8,3712]{1,0:T(8,128)S(1)}, u32[]{:S(2)}, u32[]{:S(2)}) %collective-permute-start.3) | collective-permute-done | bytes 118816 | tf_op jit(solution)/shard_map/ppermute | solution.py:31
  270.6 10.6 %all-to-all-done = f32[8,1,87552]{2,1,0:T(1,128)} async-done(((f32[8,1,87552]{2,1,0:T(1,128)}), f32[8,1,87552]{2,1,0:T(1,128)}, u32[]{:S(2)}, u32[]{:S(2)}) %all-to-all-start) | async-done | bytes 2801696 | tf_op jit(solution)/shard_map/all_to_all | solution.py:42
  281.2 3.8 %reduce_sum.69 = f32[87552]{0:T(1024)S(1)} reduce(f32[8,1,87552]{2,1,0:T(1,128)} %all-to-all-done, f32[]{:T(128)} %constant.13.clone.1), dimensions={0,1}, to_apply=%region_13.14 | reduce | flops 612864 | bytes 3151876 | tf_op jit(solution)/shard_map/reduce_sum | solution.py:47
  (139 shorter events, 68.0 us)
Async XLA Ops:
  7.2 28.4 %copy-start = (bf16[768,1536]{1,0:T(8,128)(2,1)S(1)}, bf16[768,1536]{1,0:T(8,128)(2,1)}, u32[]{:S(2)}) copy-start(bf16[768,1536]{1,0:T(8,128)(2,1)} %param.14) | copy-start | bytes 7077892
  7.2 105.2 %reduce-scatter.11.cloned.1.call-start = ((), (), s32[]{:S(2)}) async-start(), calls=%async_computation.6 | async-start | bytes 5308416 | tf_op jit(solution)/shard_map/reduce_scatter | solution.py:36
  9.2 6.9 %collective-permute-start = (bf16[2,8,3712]{2,1,0:T(8,128)(2,1)S(1)}, bf16[2,8,3712]{2,1,0:T(8,128)(2,1)S(1)}, u32[]{:S(2)}, u32[]{:S(2)}) collective-permute-start(bf16[2,8,3712]{2,1,0:T(8,128)(2,1)S(1)} %get-tuple-element.36), channel_id=1, source_target_pairs={{0,1},{1,2},{2,3},{3,4},{4,5},{5,6},{6,7},{7,8},{8,9},{9,10},{10,1... | collective-permute-start | bytes 356360 | tf_op jit(solution)/shard_map/ppermute | solution.py:19
  13.3 5.6 %collective-permute-start.1 = (bf16[2,8,3712]{2,1,0:T(8,128)(2,1)S(1)}, bf16[2,8,3712]{2,1,0:T(8,128)(2,1)S(1)}, u32[]{:S(2)}, u32[]{:S(2)}) collective-permute-start(bf16[2,8,3712]{2,1,0:T(8,128)(2,1)S(1)} %get-tuple-element.37), channel_id=1, source_target_pairs={{1,0},{2,1},{3,2},{4,3},{5,4},{6,5},{7,6},{8,7},{9,8},{10,9},{11,1... | collective-permute-start | bytes 356360 | tf_op jit(solution)/shard_map/ppermute | solution.py:21
  15.3 7.5 %copy-start.25 = (s32[320]{0:T(512)}, s32[320]{0:T(512)S(1)}, u32[]{:S(2)}) copy-start(s32[320]{0:T(512)S(1)} %get-tuple-element.38) | copy-start | bytes 3844
  16.1 21.2 %copy-start.19 = (f32[320]{0:T(512)}, f32[320]{0:T(512)S(1)}, u32[]{:S(2)}) copy-start(f32[320]{0:T(512)S(1)} %get-tuple-element.4) | copy-start | bytes 3844
  16.1 21.2 %copy-start.23 = (f32[320]{0:T(512)}, f32[320]{0:T(512)S(1)}, u32[]{:S(2)}) copy-start(f32[320]{0:T(512)S(1)} %get-tuple-element.7) | copy-start | bytes 3844
  16.2 45.8 %copy-start.21 = (f32[320]{0:T(512)}, f32[320]{0:T(512)S(1)}, u32[]{:S(2)}) copy-start(f32[320]{0:T(512)S(1)} %get-tuple-element.5) | copy-start | bytes 3844
  45.7 112.6 %reduce-scatter.9.cloned.1.call-start = ((), (), s32[]{:S(2)}) async-start(), calls=%async_computation.5 | async-start | bytes 3612672 | tf_op jit(solution)/shard_map/reduce_scatter | solution.py:36
  56.0 4.5 %copy-start.27 = (bf16[640,1280]{1,0:T(8,128)(2,1)S(1)}, bf16[640,1280]{1,0:T(8,128)(2,1)}, u32[]{:S(2)}) copy-start(bf16[640,1280]{1,0:T(8,128)(2,1)} %param.15) | copy-start | bytes 4915204
  82.1 126.3 %reduce-scatter.15.cloned.1.call-start = ((), (), s32[]{:S(2)}) async-start(), calls=%async_computation.8 | async-start | bytes 3686400 | tf_op jit(solution)/shard_map/reduce_scatter | solution.py:36
  87.8 5.4 %copy-start.16 = (bf16[320,640]{1,0:T(8,128)(2,1)S(1)}, bf16[320,640]{1,0:T(8,128)(2,1)}, u32[]{:S(2)}) copy-start(bf16[320,640]{1,0:T(8,128)(2,1)} %get-tuple-element.19) | copy-start | bytes 1228804
  87.8 146.6 %reduce-scatter.13.cloned.1.call-start = ((), (), s32[]{:S(2)}) async-start(), calls=%async_computation.7 | async-start | bytes 737280 | tf_op jit(solution)/shard_map/reduce_scatter | solution.py:36
  89.7 3.5 %copy-start.17 = (bf16[320,640]{1,0:T(8,128)(2,1)S(1)}, bf16[320,640]{1,0:T(8,128)(2,1)}, u32[]{:S(2)}) copy-start(bf16[320,640]{1,0:T(8,128)(2,1)} %get-tuple-element.20) | copy-start | bytes 1228804
  89.7 3.5 %copy-start.18 = (bf16[320,640]{1,0:T(8,128)(2,1)S(1)}, bf16[320,640]{1,0:T(8,128)(2,1)}, u32[]{:S(2)}) copy-start(bf16[320,640]{1,0:T(8,128)(2,1)} %get-tuple-element.21) | copy-start | bytes 1228804
  89.8 3.5 %copy-start.28 = (bf16[640,1280]{1,0:T(8,128)(2,1)S(1)}, bf16[640,1280]{1,0:T(8,128)(2,1)}, u32[]{:S(2)}) copy-start(bf16[640,1280]{1,0:T(8,128)(2,1)} %param.15) | copy-start | bytes 4915204
  93.2 2.7 copy-start.7
  93.3 2.7 copy-start.9
  96.0 16.4 %copy-start.20 = (f32[320]{0:T(512)S(1)}, f32[320]{0:T(512)}, u32[]{:S(2)}) copy-start(f32[320]{0:T(512)} %copy-done.19) | copy-start | bytes 3844
  223.5 7.4 %collective-permute-start.4 = (f32[12,896]{1,0:T(8,128)S(1)}, f32[12,896]{1,0:T(8,128)S(1)}, u32[]{:S(2)}, u32[]{:S(2)}) collective-permute-start(f32[12,896]{1,0:T(8,128)S(1)} %slice.180), channel_id=1, source_target_pairs={{0,1},{1,2},{2,3},{4,5},{5,6},{6,7},{8,9},{9,10},{10,11},{12,13},{... | collective-permute-start | bytes 129032
  227.7 5.0 %collective-permute-start.5 = (f32[12,1280]{1,0:T(8,128)S(1)}, f32[12,1280]{1,0:T(8,128)S(1)}, u32[]{:S(2)}, u32[]{:S(2)}) collective-permute-start(f32[12,1280]{1,0:T(8,128)S(1)} %slice.181), channel_id=1, source_target_pairs={{0,1},{1,2},{2,3},{4,5},{5,6},{6,7},{8,9},{9,10},{10,11},{12,13},{... | collective-permute-start | bytes 184328
  238.5 42.7 %all-to-all-start = ((f32[8,1,87552]{2,1,0:T(1,128)}), f32[8,1,87552]{2,1,0:T(1,128)}, u32[]{:S(2)}, u32[]{:S(2)}) async-start(f32[8,1,87552]{2,1,0:T(1,128)} %broadcast_in_dim.11), calls=%async_computation.4 | async-start | bytes 5603328 | tf_op jit(solution)/shard_map/all_to_all | solution.py:42
  259.5 6.5 %collective-permute-start.2 = (f32[8,3712]{1,0:T(8,128)S(1)}, f32[8,3712]{1,0:T(8,128)S(1)}, u32[]{:S(2)}, u32[]{:S(2)}) collective-permute-start(f32[8,3712]{1,0:T(8,128)S(1)} %get-tuple-element.32), channel_id=1, source_target_pairs={{0,1},{1,2},{2,3},{3,4},{4,5},{5,6},{6,7},{7,8},{8,9},{9,10},{10,1... | collective-permute-start | bytes 356360 | tf_op jit(solution)/shard_map/ppermute | solution.py:31
  263.5 6.4 %collective-permute-start.3 = (f32[8,3712]{1,0:T(8,128)S(1)}, f32[8,3712]{1,0:T(8,128)S(1)}, u32[]{:S(2)}, u32[]{:S(2)}) collective-permute-start(f32[8,3712]{1,0:T(8,128)S(1)} %get-tuple-element.33), channel_id=1, source_target_pairs={{1,0},{2,1},{3,2},{4,3},{5,4},{6,5},{7,6},{8,7},{9,8},{10,9},{11,1... | collective-permute-start | bytes 356360 | tf_op jit(solution)/shard_map/ppermute | solution.py:31
  (16 other events, 20.0 us)
Sparse Core Ops, SparseCore 0:
  45.9 66.4 reduce-scatter.10
  114.9 43.3 reduce-scatter.8
  160.9 47.4 reduce-scatter.14
  211.0 23.4 reduce-scatter.12
where the time goes:
time: 295 us; the launch traced here: 294 us
  waiting for transfers between devices  128 us (43%)
  other arithmetic  42.8 us (15%)
  local copies, waits for them, and re-layouts  40.8 us (14%)
  matrix products  27.4 us (9%)
  starting transfers between devices  24.3 us (8%)
  blocking collectives  15.1 us (5%)
  between operations  15 us (5%)
    reduce_scatter x4, waiting for transfers between devices, own_rows_2(): running = lax.psum_scatter(running, axis, scatter_dimension=0, tiled=True)  108 us
    unnamed x1, blocking collectives  15.1 us
    dot_general x3, matrix products, contract_rows(): lax.dot_general(first, second, (((0,), (0,)), ((), ())), preferred_elemen...  12.7 us
    all_to_all x1, waiting for transfers between devices, from_everyone(): return lax.all_to_all(copies, axis, split_axis=0, concat_axis=0, tiled=True)  10.6 us
    dot_general x3, matrix products, contract_cols(): lax.dot_general(first, weight, (((1,), (1,)), ((), ())), preferred_elemen...  9.11 us
    mul x5, local copies, waits for them, and re-layouts, edge_terms(): upstream * forward  8.89 us
    all_to_all x1, starting transfers between devices, from_everyone(): return lax.all_to_all(copies, axis, split_axis=0, concat_axis=0, tiled=True)  8.71 us
    scatter-add x1, other arithmetic, shards(): jnp.zeros((atom_count + 2 * reach, row_width), jnp.float32).at[src_local]  8.57 us
  transfers between devices with their start and end apart: 11, of which 9 were waited for; matrix products, arithmetic and copies ran while one was open for 29% of the time, Pallas kernels for 0%

commit v1 on v0

v1 whole, which is shorter than its diff:
```python
import functools

import jax
import jax.numpy as jnp
from jax import lax
from jax.experimental import pallas as pl
from jax.experimental.pallas import tpu as pltpu
from jax.sharding import PartitionSpec as P

MESH = pl.DeviceIdType.MESH
F32 = jnp.float32
BF16 = jnp.bfloat16
HEADS = 8
LANES = 128
EDGES = 320
PADDED = 384
BLOCKS = 29
ZERO, ONE, TWO = 7, 6, 5
AT_Z, AT_P1, AT_N1, AT_P2, AT_N2 = 0, 7, 13, 19, 24
VMEM_LIMIT = 62 * 1024 * 1024


def dot(a, b):
    return jnp.dot(a, b, preferred_element_type=F32)


def dot_t(a, b):
    return lax.dot_general(a, b, (((1,), (1,)), ((), ())), preferred_element_type=F32)


def dot_first(a, b):
    return lax.dot_general(a, b, (((0,), (0,)), ((), ())), preferred_element_type=F32)


def split2(v):
    high = v.astype(BF16)
    return high, (v - high.astype(F32)).astype(BF16)


def split3(v):
    high = v.astype(BF16)
    rest = v - high.astype(F32)
    middle = rest.astype(BF16)
    return high, middle, (rest - middle.astype(F32)).astype(BF16)


def chunks(count):
    out, at = [], 0
    while at < count:
        width = min(2, count - at)
        out.append((at, width))
        at += width
    return out


def cols(block, width=1):
    return pl.ds(block * LANES, width * LANES)


def wide(v, width):
    return v if width == 1 else jnp.concatenate([v] * width, axis=1)


def folded(v, width):
    return v if width == 1 else v[:, :LANES] + v[:, LANES:]


def edge_kernel(rows_ref, tab_ref, w0_ref, w1_ref, w2_ref, xt_ref, d_ref, node_ref, x_s, du_s, trig_s, oh_s):
    rows = rows_ref[...]
    parts = jnp.concatenate(list(split3(rows)), axis=0)
    pick_row = lax.broadcasted_iota(jnp.int32, (24, 6 * LANES), 0)
    pick_col = lax.broadcasted_iota(jnp.int32, (24, 6 * LANES), 1)
    chosen = jnp.where(pick_row % 8 == pick_col // LANES, 1.0, 0.0).astype(BF16)
    spread = dot_first(parts, chosen)
    for k in range(4):
        trig_s[k] = spread[:, k * LANES : (k + 1) * LANES]
    lane = lax.broadcasted_iota(jnp.int32, (EDGES, LANES), 1).astype(F32)
    for k in range(2):
        oh_s[k] = jnp.where(spread[:, (4 + k) * LANES : (5 + k) * LANES] == lane, 1.0, 0.0).astype(BF16)
    depth = tab_ref.shape[0]
    oh_src = oh_s[0, :, :depth]
    oh_dst = oh_s[1, :, :depth]

    xt_ref[:, :, EDGES:] = jnp.zeros((BLOCKS, LANES, PADDED - EDGES), BF16)
    d_ref[:, EDGES:, :] = jnp.zeros((BLOCKS, PADDED - EDGES, LANES), BF16)

    def keep_x(block, width, v):
        x_s[:, cols(block, width)] = v
        for w in range(width):
            xt_ref[block + w, :, :EDGES] = v[:, w * LANES : (w + 1) * LANES].T

    def rotated(onehot, c, s, plus, minus, width):
        a = dot(onehot, tab_ref[:, cols(plus, width)])
        b = dot(onehot, tab_ref[:, cols(minus, width)])
        return c * a - s * b, s * a + c * b

    for at, width in chunks(ZERO):
        keep_x(at, width, dot(oh_src, tab_ref[:, cols(at, width)]).astype(BF16))
    for m, (count, plus, minus) in enumerate(((ONE, AT_P1, AT_N1), (TWO, AT_P2, AT_N2))):
        for at, width in chunks(count):
            c, s = wide(trig_s[2 * m], width), wide(trig_s[2 * m + 1], width)
            p, n = rotated(oh_src, c, s, plus + at, minus + at, width)
            keep_x(plus + at, width, p.astype(BF16))
            keep_x(minus + at, width, n.astype(BF16))

    total = jnp.zeros((EDGES, LANES), F32)
    first = None
    for at, width in chunks(ZERO):
        out = dot(x_s[:, cols(0, ZERO)], w0_ref[:, cols(at, width)])
        if at == 0:
            first = out[:, :LANES]
        up = dot(oh_dst, tab_ref[:, cols(at, width)])
        du_s[:, cols(at, width)] = up
        total = total + folded(up * out, width)
    for m, (count, plus, minus, w_ref) in enumerate(((ONE, AT_P1, AT_N1, w1_ref), (TWO, AT_P2, AT_N2, w2_ref))):
        for at, width in chunks(count):
            c, s = wide(trig_s[2 * m], width), wide(trig_s[2 * m + 1], width)
            up_p, up_n = rotated(oh_dst, c, s, plus + at, minus + at, width)
            du_s[:, cols(plus + at, width)] = up_p
            du_s[:, cols(minus + at, width)] = up_n
            xp, xn = x_s[:, cols(plus, count)], x_s[:, cols(minus, count)]
            left, right = w_ref[:, cols(at, width)], w_ref[:, cols(count + at, width)]
            out_p = dot(xp, left) - dot(xn, right)
            out_n = dot(xp, right) + dot(xn, left)
            total = total + folded(up_p * out_p + up_n * out_n, width)

    size = LANES // HEADS
    head_r = lax.broadcasted_iota(jnp.int32, (LANES, LANES), 0) // size
    head_c = lax.broadcasted_iota(jnp.int32, (LANES, LANES), 1) // size
    same = jnp.where(head_r == head_c, 1.0, 0.0).astype(BF16)

    def head_sum(v):
        high, middle, low = split3(v)
        return dot(low, same) + dot(middle, same) + dot(high, same)

    scale = 1.0 / (float(size) ** 0.5)
    gate = jax.nn.sigmoid(head_sum(first) * scale)
    dlogit = head_sum(total) * gate * (1.0 - gate) * scale
    for block in range(BLOCKS):
        v = du_s[:, cols(block)] * gate
        if block == 0:
            v = v + dlogit
        d_ref[block, :EDGES, :] = v.astype(BF16)

    atoms = node_ref.shape[0]
    atom = lax.broadcasted_iota(jnp.int32, (atoms, EDGES), 0)
    table_row = jnp.where(atom < 8, atom + 32, jnp.where(atom < 16, atom - 8, jnp.where(atom < 24, atom, atom + 24)))
    oh_rows = jnp.where(table_row.astype(F32) == rows[4:5, :], 1.0, 0.0).astype(BF16)

    def scatter(block, width, v):
        high, low = split2(v)
        node_ref[:, cols(block, width)] = dot(oh_rows, high) + dot(oh_rows, low)

    def dconv(block, count):
        return jnp.concatenate([d_ref[block + k, :EDGES, :] for k in range(count)], axis=1)

    dz = dconv(AT_Z, ZERO)
    for at, width in chunks(ZERO):
        scatter(at, width, dot_t(dz, w0_ref[cols(at, width), :]))
    for m, (count, plus, minus, w_ref) in enumerate(((ONE, AT_P1, AT_N1, w1_ref), (TWO, AT_P2, AT_N2, w2_ref))):
        dp, dn = dconv(plus, count), dconv(minus, count)
        for at, width in chunks(count):
            c, s = wide(trig_s[2 * m], width), wide(trig_s[2 * m + 1], width)
            left, right = w_ref[cols(at, width), cols(0, count)], w_ref[cols(at, width), cols(count, count)]
            back_p = dot_t(dp, left) + dot_t(dn, right)
            back_n = dot_t(dn, left) - dot_t(dp, right)
            scatter(plus + at, width, c * back_p + s * back_n)
            scatter(minus + at, width, c * back_n - s * back_p)


def edge_call(rows, table, w_zero, w_one, w_two):
    width = table.shape[1]
    vmem = pl.BlockSpec(memory_space=pltpu.VMEM)
    return pl.pallas_call(
        edge_kernel,
        out_shape=(
            jax.ShapeDtypeStruct((BLOCKS, LANES, PADDED), BF16),
            jax.ShapeDtypeStruct((BLOCKS, PADDED, LANES), BF16),
            jax.ShapeDtypeStruct((32, width), F32),
        ),
        in_specs=[vmem] * 5,
        out_specs=(vmem,) * 3,
        scratch_shapes=[
            pltpu.VMEM((EDGES, width), BF16),
            pltpu.VMEM((EDGES, width), F32),
            pltpu.VMEM((4, EDGES, LANES), F32),
            pltpu.VMEM((2, EDGES, LANES), BF16),
        ],
        compiler_params=pltpu.CompilerParams(vmem_limit_bytes=VMEM_LIMIT),
        name="edge_terms",
    )(rows, table, w_zero, w_one, w_two)


SHARES = (
    ((0, 7, 29), (1, 7, 21), (1, 24, 26)),
    ((0, 0, 7), (0, 19, 29), (1, 0, 7), (1, 21, 24), (1, 26, 29)),
)
ONE_ORDER = tuple(b for j in range(3) for b in (2 * j, 2 * j + 1, 6 + 2 * j, 7 + 2 * j))
TILES = (
    tuple((1, i, b) for b in ONE_ORDER for i in range(3)) + tuple((2, i, b) for b in (0, 1, 5, 6) for i in range(3)),
    tuple((0, i, b) for b in range(7) for i in range(4)) + tuple((2, i, b) for b in (2, 3, 4, 7, 8, 9) for i in range(3)),
)
PLACE = tuple({tile: at for at, tile in enumerate(order)} for order in TILES)
NX, NY, NZ, NK = 4, 4, 8, 4
AXES = (("z", "x", "y"), ("x", "y", "z"), ("y", "z", "x"))
COUNT = {"x": NX, "y": NY, "z": NZ}


def chains_of(n):
    return ((1, 0, n // 2), (-1, 1, n // 2), (1, 1, n // 2 - 1), (-1, 0, n // 2 - 1))


def reduce_kernel(
    xt_ref, d_ref, node_ref,
    nodes_out, zero_out, one_out, two_out,
    xt_s, d_s, part0, part1, part2, r10, r11, r12, s20, s21, s22, r20, r21, r22, s30, s31, s32, r30, r31, r32,
    gathered, result, node_in,
    load_sem, share_send, share_recv, send1, recv1, send2, recv2, send3, recv3, all_send, all_recv, node_send, node_recv,
):
    dp = lax.axis_index("dp")
    graph = lax.axis_index("graph")
    core, x = dp % 2, dp // 2
    y, z = graph % NY, graph // NY
    place = {"x": x, "y": y, "z": z}

    def moved(axis, offset):
        n = COUNT[axis]
        to = (place[axis] + offset + n) % n
        if axis == "x":
            return {"dp": to * 2 + core, "graph": graph}
        if axis == "y":
            return {"dp": dp, "graph": z * NY + to}
        return {"dp": dp, "graph": to * NY + y}

    sibling = {"dp": x * 2 + (1 - core), "graph": graph}
    graphs = NY * NZ
    before = {"dp": dp, "graph": (graph + graphs - 1) % graphs}
    after = {"dp": dp, "graph": (graph + 1) % graphs}
    peers = [{"dp": (dp + o) % 8, "graph": graph} for o in range(1, 8)]
    peers += [moved("y", o) for o in range(1, NY)] + [moved("z", o) for o in range(1, NZ)] + [before, after]

    barrier = pltpu.get_barrier_semaphore()
    for peer in peers:
        pl.semaphore_signal(barrier, inc=1, device_id=peer, device_id_type=MESH)
    pl.semaphore_wait(barrier, len(peers))

    def remote(src, dst, send, recv, device):
        return pltpu.make_async_remote_copy(
            src_ref=src, dst_ref=dst, send_sem=send, recv_sem=recv, device_id=device, device_id_type=MESH
        )

    node_up = remote(node_ref.at[pl.ds(0, 8)], node_in.at[1], node_send.at[0], node_recv.at[0], before)
    node_down = remote(node_ref.at[pl.ds(24, 8)], node_in.at[0], node_send.at[1], node_recv.at[1], after)

    def own_half(kind, lo, hi, half):
        if kind == 0:
            return xt_s.at[pl.ds(lo, hi - lo), :, pl.ds(half * PADDED, PADDED)]
        return d_s.at[pl.ds(lo, hi - lo), pl.ds(half * PADDED, PADDED), :]

    def source_of(kind, lo, hi):
        return (d_ref if kind else xt_ref).at[pl.ds(lo, hi - lo)]

    def share_copy(k, span):
        return remote(source_of(*span), own_half(*span, 1), share_send.at[k], share_recv.at[k], sibling)

    def load_copy(k, span):
        return pltpu.make_async_copy(source_of(*span), own_half(*span, 0), load_sem.at[k])

    stage1 = (part0, part1, part2)
    rings1 = (r10, r11, r12)
    stage2 = (s20, s21, s22)
    rings2 = (r20, r21, r22)
    stage3 = (s30, s31, s32)
    slots3 = (r30, r31, r32)

    def slot_of(n, chain, step):
        return sum(c[2] for c in chains_of(n)[:chain]) + step

    def ring_copy(part, stage, chain, step):
        axis = AXES[part][stage]
        n = COUNT[axis]
        way, half, steps = chains_of(n)[chain]
        source, ring = ((stage1, rings1), (stage2, rings2))[stage]
        sends, recvs = ((send1, recv1), (send2, recv2))[stage]
        deep = source[part].shape[1] // 2
        slot = slot_of(n, chain, step)
        if step == 0:
            block = (place[axis] + way * steps + n) % n
            src = source[part].at[block, pl.ds(half * deep, deep)]
        else:
            src = ring[part].at[slot - 1]
        return remote(src, ring[part].at[slot], sends.at[part, slot], recvs.at[part, slot], moved(axis, way))

    def begin(part, stage):
        for chain in range(4):
            ring_copy(part, stage, chain, 0).start()

    def advance(part, stage, step):
        axis = AXES[part][stage]
        n = COUNT[axis]
        source, ring = ((stage1, rings1), (stage2, rings2))[stage]
        deep = source[part].shape[1] // 2
        for chain, (way, half, steps) in enumerate(chains_of(n)):
            if step < steps:
                slot = slot_of(n, chain, step)
                ring_copy(part, stage, chain, step - 1).wait_recv()
                block = (place[axis] + way * (steps - step) + n) % n
                ring[part][slot - 1] = ring[part][slot - 1] + source[part][block, pl.ds(half * deep, deep)]
                ring_copy(part, stage, chain, step).start()

    def finish(part, stage, out):
        axis = AXES[part][stage]
        n = COUNT[axis]
        source, ring = ((stage1, rings1), (stage2, rings2))[stage]
        deep = source[part].shape[1] // 2
        for half in range(2):
            arrived = []
            for chain, (way, h, steps) in enumerate(chains_of(n)):
                if h == half:
                    ring_copy(part, stage, chain, steps - 1).wait_recv()
                    arrived.append(ring[part][slot_of(n, chain, steps - 1)])
            out[pl.ds(half * deep, deep)] = source[part][place[axis], pl.ds(half * deep, deep)] + arrived[0] + arrived[1]

    def sent(part, stage):
        for chain, (way, half, steps) in enumerate(chains_of(COUNT[AXES[part][stage]])):
            for step in range(steps):
                ring_copy(part, stage, chain, step).wait_send()

    def last_copy(part, offset):
        axis = AXES[part][2]
        n = COUNT[axis]
        return remote(
            stage3[part].at[(place[axis] + offset) % n], slots3[part].at[offset - 1],
            send3.at[part, offset - 1], recv3.at[part, offset - 1], moved(axis, offset),
        )

    def put(which, tile, row_y, v):
        at = PLACE[which][tile]
        part, px, pk = at // 16, (at % 16) // 4, at % 4
        if part == 0:
            part0[:, px, row_y, pk] = v
        elif part == 1:
            part1[px, row_y, :, pk] = v
        else:
            part2[row_y, :, px, pk] = v

    def pair(block, width):
        return jnp.concatenate([d_s[block + k] for k in range(width)], axis=1)

    def factor(block, count):
        return xt_s[pl.ds(block, count)].reshape(count * LANES, 2 * PADDED)

    def put_aligned(v, first_blocks):
        shaped = v.reshape(NZ, NY * 3, 8, v.shape[1])
        for w, b in enumerate(first_blocks):
            for row_y in range(NY):
                for i in range(3):
                    put(0, (1, i, b), row_y, shaped[:, row_y * 3 + i, :, w * LANES : (w + 1) * LANES])

    def put_shifted(which, matrix, tiles, shard, v, first_blocks):
        result[:, pl.ds(0, NY * shard), pl.ds(0, v.shape[1])] = v.reshape(NZ, NY * shard, v.shape[1])
        for w, b in enumerate(first_blocks):
            for row_y in range(NY):
                for i in range(tiles):
                    put(which, (matrix, i, b), row_y, result[:, pl.ds(row_y * shard + i * 8, 8), cols(w)])

    def two_blocks(which, at, width):
        dp_, dn_ = pair(AT_P2 + at, width), pair(AT_N2 + at, width)
        rp, rn = factor(AT_P2, TWO), factor(AT_N2, TWO)
        put_shifted(which, 2, 3, 20, dot(rp, dp_) + dot(rn, dn_), range(at, at + width))
        put_shifted(which, 2, 3, 20, dot(rp, dn_) - dot(rn, dp_), range(TWO + at, TWO + at + width))

    node_up.start()
    node_down.start()
    result[...] = jnp.zeros_like(result)

    @pl.when(core == 0)
    def _():
        for k, span in enumerate(SHARES[1]):
            share_copy(k, span).start()
        for k, span in enumerate(SHARES[0]):
            load_copy(k, span).start()
        for k, span in enumerate(SHARES[0]):
            load_copy(k, span).wait()
            share_copy(k, span).wait_recv()
        for j in range(3):
            dp_, dn_ = pair(AT_P1 + 2 * j, 2), pair(AT_N1 + 2 * j, 2)
            rp, rn = factor(AT_P1, ONE), factor(AT_N1, ONE)
            put_aligned(dot(rp, dp_) + dot(rn, dn_), (2 * j, 2 * j + 1))
            put_aligned(dot(rp, dn_) - dot(rn, dp_), (6 + 2 * j, 7 + 2 * j))
            if j:
                begin(j - 1, 0)
        two_blocks(0, 0, 2)
        begin(2, 0)
        for k, span in enumerate(SHARES[1]):
            share_copy(k, span).wait_send()

    @pl.when(core == 1)
    def _():
        for k, span in enumerate(SHARES[0]):
            share_copy(k, span).start()
        for k, span in enumerate(SHARES[1]):
            load_copy(k, span).start()
        for k, span in enumerate(SHARES[1]):
            load_copy(k, span).wait()
            share_copy(k, span).wait_recv()
        blank = jnp.zeros((NZ, 8, LANES), F32)
        for row_y in range(NY):
            for k in (2, 3):
                part2[row_y, :, 3, k] = blank
        for at, width in chunks(ZERO):
            put_shifted(1, 0, 4, 28, dot(factor(AT_Z, ZERO), pair(AT_Z + at, width)), range(at, at + width))
            if at == 2:
                begin(0, 0)
        two_blocks(1, 2, 2)
        begin(1, 0)
        two_blocks(1, 4, 1)
        begin(2, 0)
        for k, span in enumerate(SHARES[0]):
            share_copy(k, span).wait_send()

    node_up.wait()
    node_down.wait()
    nodes_out[pl.ds(0, 8)] = (node_ref[pl.ds(8, 8)] + node_in[0]).astype(BF16)
    nodes_out[pl.ds(8, 8)] = (node_ref[pl.ds(16, 8)] + node_in[1]).astype(BF16)

    advance(1, 0, 1)
    advance(2, 0, 1)
    advance(0, 0, 1)
    advance(0, 0, 2)
    finish(1, 0, s21)
    begin(1, 1)
    finish(2, 0, s22)
    begin(2, 1)
    advance(0, 0, 3)
    advance(1, 1, 1)
    advance(2, 1, 1)
    finish(0, 0, s20)
    begin(0, 1)
    finish(1, 1, s31)
    for offset in range(1, NZ):
        last_copy(1, offset).start()
    advance(2, 1, 2)
    advance(0, 1, 1)
    advance(2, 1, 3)
    finish(0, 1, s30)
    for offset in range(1, NY):
        last_copy(0, offset).start()
    finish(2, 1, s32)
    for offset in range(1, NX):
        last_copy(2, offset).start()
    for part in range(3):
        axis = AXES[part][2]
        sum_ = stage3[part][place[axis]]
        for offset in range(1, COUNT[axis]):
            last_copy(part, offset).wait_recv()
            sum_ = sum_ + slots3[part][offset - 1]
        gathered[dp, pl.ds(part * NK, NK)] = sum_

    def all_copy(offset):
        return remote(
            gathered.at[dp], gathered.at[dp], all_send.at[offset - 1], all_recv.at[offset - 1],
            {"dp": (dp + offset) % 8, "graph": graph},
        )

    for offset in range(1, 8):
        all_copy(offset).start()
    for part in range(3):
        sent(part, 0)
        sent(part, 1)
        for offset in range(1, COUNT[AXES[part][2]]):
            last_copy(part, offset).wait_send()
    for offset in range(1, 8):
        all_copy(offset).wait_recv()
    outs = (zero_out, one_out, two_out)
    for which in range(2):
        for at, (matrix, i, b) in enumerate(TILES[which]):
            part, px, pk = at // 16, (at % 16) // 4, at % 4
            out = outs[matrix]
            rows = min(8, out.shape[0] - 8 * i)
            out[pl.ds(8 * i, rows), cols(b)] = gathered[px * 2 + which, part * NK + pk, pl.ds(0, rows)] * 0.125
    for offset in range(1, 8):
        all_copy(offset).wait_send()


def reduce_call(xt, d, node):
    width = node.shape[1]
    vmem = pl.BlockSpec(memory_space=pltpu.VMEM)
    hbm = pl.BlockSpec(memory_space=pl.ANY)
    tile = (NK, 8, LANES)
    dims = [[COUNT[a] for a in axes] for axes in AXES]

    def ring(part, stage):
        n = dims[part][stage]
        inner = dims[part][stage + 1 :]
        return pltpu.VMEM((2 * (n - 1), inner[0] // 2, *inner[1:], *tile), F32)

    dma = pltpu.SemaphoreType.DMA
    return pl.pallas_call(
        reduce_kernel,
        out_shape=(
            jax.ShapeDtypeStruct((16, width), BF16),
            jax.ShapeDtypeStruct((28, ZERO * LANES), F32),
            jax.ShapeDtypeStruct((24, 2 * ONE * LANES), F32),
            jax.ShapeDtypeStruct((20, 2 * TWO * LANES), F32),
        ),
        in_specs=[hbm, hbm, vmem],
        out_specs=(vmem,) * 4,
        scratch_shapes=[
            pltpu.VMEM((BLOCKS, LANES, 2 * PADDED), BF16),
            pltpu.VMEM((BLOCKS, 2 * PADDED, LANES), BF16),
            *[pltpu.VMEM((*dims[p], *tile), F32) for p in range(3)],
            *[ring(p, 0) for p in range(3)],
            *[pltpu.VMEM((*dims[p][1:], *tile), F32) for p in range(3)],
            *[ring(p, 1) for p in range(3)],
            *[pltpu.VMEM((dims[p][2], *tile), F32) for p in range(3)],
            *[pltpu.VMEM((dims[p][2] - 1, *tile), F32) for p in range(3)],
            pltpu.VMEM((8, 3 * NK, 8, LANES), F32),
            pltpu.VMEM((NZ, 120, 2 * LANES), F32),
            pltpu.VMEM((2, 8, width), F32),
            dma((5,)), dma((5,)), dma((5,)),
            dma((3, 14)), dma((3, 14)), dma((3, 14)), dma((3, 14)), dma((3, 7)), dma((3, 7)),
            dma((7,)), dma((7,)), dma((2,)), dma((2,)),
        ],
        compiler_params=pltpu.CompilerParams(
            vmem_limit_bytes=VMEM_LIMIT, collective_id=0, has_side_effects=True
        ),
        name="weight_sums",
    )(xt, d, node)


def shards(node_feats, node_cotan, source, target, angle, w_zero, w_one, w_two):
    graphs = lax.axis_size("graph")
    atoms = node_feats.shape[1]
    reach = atoms // 2
    position = lax.axis_index("graph")
    feats, cotan = node_feats[0], node_cotan[0]
    own_low = jnp.concatenate([feats[:reach], cotan[:reach]], 0)
    own_high = jnp.concatenate([feats[reach:], cotan[reach:]], 0)
    from_before = lax.ppermute(own_high, "graph", [(i, (i + 1) % graphs) for i in range(graphs)])
    from_after = lax.ppermute(own_low, "graph", [((i + 1) % graphs, i) for i in range(graphs)])
    table = jnp.concatenate([own_low, own_high, from_before, from_after], 0)

    def table_row(atom):
        local = atom - (position * atoms - reach)
        block = local // reach
        start = jnp.where(block == 0, 32, jnp.where(block == 1, 0, jnp.where(block == 2, 16, 48)))
        return (start + local % reach).astype(F32)

    phases = angle[0]
    zero = jnp.zeros_like(phases)
    rows = jnp.stack(
        [
            jnp.cos(phases), jnp.sin(phases), jnp.cos(2.0 * phases), jnp.sin(2.0 * phases),
            table_row(source[0]), table_row(target[0]) + reach, zero, zero,
        ],
        0,
    )
    xt, d, node = edge_call(rows, table, w_zero, w_one, w_two)
    nodes, zero_g, one_g, two_g = reduce_call(xt, d, node)
    return nodes[None], zero_g, one_g, two_g


def solution(mesh):
    placed = (
        P("dp", "graph", None),
        P("dp", "graph", None),
        P("dp", "graph"),
        P("dp", "graph"),
        P("dp", "graph"),
        P(),
        P(),
        P(),
    )
    return jax.shard_map(
        shards,
        mesh=mesh,
        in_specs=placed,
        out_specs=(P("dp", "graph", None), P("graph", None), P("graph", None), P("graph", None)),
        check_vma=False,
    )
```

time: 295 us -> 105 us (0.36)
  waiting for transfers between devices: 128 us -> 0.01 us
  Pallas kernels: 0 us -> 80.9 us
  other arithmetic: 42.8 us -> 2.22 us
  local copies, waits for them, and re-layouts: 40.8 us -> 11.9 us
  matrix products: 27.4 us -> 0 us
  starting transfers between devices: 24.3 us -> 9.02 us
  blocking collectives: 15.1 us -> 0 us
  between operations: 15 us -> 0.68 us
    reduce_scatter x4 -> x0, waiting for transfers between devices: 108 us -> none  [own_rows_2(): running = lax.psum_scatter(running, axis, scatter_dimension=0, tiled=True)]
    pallas_call x0 -> x2, Pallas kernels: none -> 80.9 us  [the longest x1 63.2 us: reduce_call(): pl.pallas_call(reduce_kernel, out_shape=(jax.ShapeDtypeStruct((16, width)...]
    dot_general x9 -> x0, matrix products: 27.4 us -> none  [the longest x3 12.7 us: contract_rows(): lax.dot_general(first, second, (((0,), (0,)), ((), ())), preferred_elemen...]
    mul x11 -> x0, local copies, waits for them, and re-layouts: 16.8 us -> none  [the longest x5 8.89 us: edge_terms(): upstream * forward]
    unnamed x1 -> x0, blocking collectives: 15.1 us -> none
    all_to_all x1 -> x0, waiting for transfers between devices: 10.6 us -> none  [from_everyone(): return lax.all_to_all(copies, axis, split_axis=0, concat_axis=0, tiled=True)]
    all_to_all x1 -> x0, starting transfers between devices: 8.71 us -> none  [from_everyone(): return lax.all_to_all(copies, axis, split_axis=0, concat_axis=0, tiled=True)]
    reduce_sum x7 -> x0, other arithmetic: 8.61 us -> none  [the longest x5 4.78 us: edge_terms(): per_head(upstream * forward, channels, heads).sum(axis=(1, 3))]
  transfers between devices with their start and end apart: 11 -> 2, of which waited for: 9 -> 0; matrix products, arithmetic and copies ran while one was open for 29% -> 6% of each run, Pallas kernels for 0% -> 0%
where the time goes in v1:
time: 105 us
  Pallas kernels  80.9 us (77%)
  local copies, waits for them, and re-layouts  11.9 us (11%)
  starting transfers between devices  9.02 us (9%)
  other arithmetic  2.22 us (2%)
    pallas_call x1, Pallas kernels, reduce_call(): pl.pallas_call(reduce_kernel, out_shape=(jax.ShapeDtypeStruct((16, width)...  63.2 us
    pallas_call x1, Pallas kernels, edge_call(): pl.pallas_call(edge_kernel, out_shape=(jax.ShapeDtypeStruct((BLOCKS, LANE...  17.7 us
    unnamed x11, local copies, waits for them, and re-layouts  10.4 us
    ppermute x1, starting transfers between devices, shards(): lax.ppermute(own_low, 'graph', [((i + 1) % graphs, i) for i in range(grap...  6.82 us
    ppermute x1, starting transfers between devices, shards(): lax.ppermute(own_high, 'graph', [(i, (i + 1) % graphs) for i in range(gra...  2.2 us
  transfers between devices with their start and end apart: 2, of which 0 were waited for; matrix products, arithmetic and copies ran while one was open for 6% of the time, Pallas kernels for 0%

profile of v1, /device:TPU:1, one launch (start us, length us, event | category | flops | bytes accessed | tf_op | source)
XLA Modules:
  0.0 104.8 jit_solution(15945387533462565272)
XLA Ops:
  0.6 0.9 slice_bitcast_fusion.2
  1.6 2.2 %collective-permute-start = (bf16[16,3712]{1,0:T(8,128)(2,1)S(1)}, bf16[16,3712]{1,0:T(8,128)(2,1)S(1)}, u32[]{:S(2)}, u32[]{:S(2)}) collective-permute-start(bf16[16,3712]{1,0:T(8,128)(2,1)S(1)} %pad_maximum_fusion), channel_id=1, source_target_pairs={{0,1},{1,2},{2,3},{3,4},{4,5},{5,6},{6,7},{7,8},{8,9},{9,10},{10,1... | collective-permute-start | bytes 356360 | tf_op jit(solution)/shard_map/ppermute | solution.py:540
  3.8 6.8 %collective-permute-start.1 = (bf16[16,3712]{1,0:T(8,128)(2,1)S(1)}, bf16[16,3712]{1,0:T(8,128)(2,1)S(1)}, u32[]{:S(2)}, u32[]{:S(2)}) collective-permute-start(bf16[16,3712]{1,0:T(8,128)(2,1)S(1)} %pad_maximum_fusion.1), channel_id=1, source_target_pairs={{1,0},{2,1},{3,2},{4,3},{5,4},{6,5},{7,6},{8,7},{9,8},{10,9},{11,1... | collective-permute-start | bytes 356360 | tf_op jit(solution)/shard_map/ppermute | solution.py:541
  10.6 0.8 constant_dynamic-update-slice_fusion.5
  11.5 0.8 multiply_sine_fusion
  12.2 0.8 constant_dynamic-update-slice_fusion.4
  13.1 0.8 constant_dynamic-update-slice_fusion.3
  13.9 0.8 constant_dynamic-update-slice_fusion.2
  14.7 0.7 fusion.2
  15.4 0.7 convert_add_fusion
  16.2 0.6 stack.5.rows_ref
  16.8 0.0 collective-permute-done
  16.8 0.0 collective-permute-done.1
  16.8 0.0 copy-start
  16.8 0.8 copy-done
  17.6 17.7 %edge_terms.1 = (bf16[29,128,384]{2,1,0:T(8,128)(2,1)}, bf16[29,384,128]{2,1,0:T(8,128)(2,1)}, f32[32,3712]{1,0:T(8,128)}) custom-call(f32[8,320]{1,0:T(8,128)} %stack.5.rows_ref, bf16[64,3712]{1,0:T(8,128)(2,1)} %copy-done, bf16[896,896]{1,0:T(8,128)(2,1)} %w0_ref.1, bf16[768,1536]{1,0:T(8,128)(2,1)} %w1_ref.1, bf16[640,1280]{1,0:T(8,128)(2,1)} %w2_ref.1), custom_call_target="tpu_custom_call" | custom-call | tf_op jit(solution)/shard_map/edge_terms/pallas_call | solution.py:174
  35.3 63.2 %weight_sums.1 = (bf16[16,3712]{1,0:T(8,128)(2,1)}, f32[28,896]{1,0:T(8,128)}, f32[24,1536]{1,0:T(8,128)}, f32[20,1280]{1,0:T(8,128)}) custom-call(bf16[29,128,384]{2,1,0:T(8,128)(2,1)} %get-tuple-element.11.xt_ref, bf16[29,384,128]{2,1,0:T(8,128)(2,1)} %get-tuple-element.12.d_ref, f32[32,3712]{1,0:T(8,128)} %get-tuple-element.13.node_ref), custom_call_target="tpu_custom_call" | custom-call | tf_op jit(solution)/shard_map/weight_sums/pallas_call | solution.py:499
  98.5 1.6 %copy.21 = bf16[1,16,3712]{2,1,0:T(8,128)(2,1)} copy(bf16[1,16,3712]{2,1,0:T(8,128)(2,1)} %bitcast.17) | data formatting | bytes 237568
  100.1 1.6 %copy.22 = f32[28,896]{1,0:T(8,128)} copy(f32[28,896]{1,0:T(8,128)} %get-tuple-element.33) | data formatting | bytes 200704
  101.6 1.6 %copy.23 = f32[24,1536]{1,0:T(8,128)} copy(f32[24,1536]{1,0:T(8,128)} %get-tuple-element.34) | data formatting | bytes 294912
  103.2 1.6 %copy.24 = f32[20,1280]{1,0:T(8,128)} copy(f32[20,1280]{1,0:T(8,128)} %get-tuple-element.35) | data formatting | bytes 204800
  (5 shorter events, 0.1 us)
Async XLA Ops:
  1.6 15.2 %collective-permute-start = (bf16[16,3712]{1,0:T(8,128)(2,1)S(1)}, bf16[16,3712]{1,0:T(8,128)(2,1)S(1)}, u32[]{:S(2)}, u32[]{:S(2)}) collective-permute-start(bf16[16,3712]{1,0:T(8,128)(2,1)S(1)} %pad_maximum_fusion), channel_id=1, source_target_pairs={{0,1},{1,2},{2,3},{3,4},{4,5},{5,6},{6,7},{7,8},{8,9},{9,10},{10,1... | collective-permute-start | bytes 356360 | tf_op jit(solution)/shard_map/ppermute | solution.py:540
  3.8 13.0 %collective-permute-start.1 = (bf16[16,3712]{1,0:T(8,128)(2,1)S(1)}, bf16[16,3712]{1,0:T(8,128)(2,1)S(1)}, u32[]{:S(2)}, u32[]{:S(2)}) collective-permute-start(bf16[16,3712]{1,0:T(8,128)(2,1)S(1)} %pad_maximum_fusion.1), channel_id=1, source_target_pairs={{1,0},{2,1},{3,2},{4,3},{5,4},{6,5},{7,6},{8,7},{9,8},{10,9},{11,1... | collective-permute-start | bytes 356360 | tf_op jit(solution)/shard_map/ppermute | solution.py:541
  16.8 0.8 copy-start

commit v2 on v1

v2 whole, which is shorter than its diff:
```python
import jax
import jax.numpy as jnp
from jax import lax
from jax.experimental import pallas as pl
from jax.experimental.pallas import tpu as pltpu
from jax.sharding import PartitionSpec as P

MESH = pl.DeviceIdType.MESH
F32 = jnp.float32
BF16 = jnp.bfloat16
HEADS = 8
LANES = 128
EDGES = 320
PADDED = 384
BLOCKS = 29
ZERO, ONE, TWO = 7, 6, 5
AT_Z, AT_P1, AT_N1, AT_P2, AT_N2 = 0, 7, 13, 19, 24
VMEM_LIMIT = 62 * 1024 * 1024


def dot(a, b):
    return jnp.dot(a, b, preferred_element_type=F32)


def dot_t(a, b):
    return lax.dot_general(a, b, (((1,), (1,)), ((), ())), preferred_element_type=F32)


def dot_first(a, b):
    return lax.dot_general(a, b, (((0,), (0,)), ((), ())), preferred_element_type=F32)


def split2(v):
    high = v.astype(BF16)
    return high, (v - high.astype(F32)).astype(BF16)


def split3(v):
    high = v.astype(BF16)
    rest = v - high.astype(F32)
    middle = rest.astype(BF16)
    return high, middle, (rest - middle.astype(F32)).astype(BF16)


def chunks(count):
    out, at = [], 0
    while at < count:
        width = min(2, count - at)
        out.append((at, width))
        at += width
    return out


def cols(block, width=1):
    return pl.ds(block * LANES, width * LANES)


def wide(v, width):
    return v if width == 1 else jnp.concatenate([v] * width, axis=1)


def folded(v, width):
    return v if width == 1 else v[:, :LANES] + v[:, LANES:]


SHARES = (
    ((0, 7, 29), (1, 7, 21), (1, 24, 26)),
    ((0, 0, 7), (0, 19, 29), (1, 0, 7), (1, 21, 24), (1, 26, 29)),
)
ONE_ORDER = tuple(b for j in range(3) for b in (2 * j, 2 * j + 1, 6 + 2 * j, 7 + 2 * j))
TILES = (
    tuple((1, i, b) for b in ONE_ORDER for i in range(3)) + tuple((2, i, b) for b in (0, 1, 5, 6) for i in range(3)),
    tuple((0, i, b) for b in range(7) for i in range(4)) + tuple((2, i, b) for b in (2, 3, 4, 7, 8, 9) for i in range(3)),
)
PLACE = tuple({tile: at for at, tile in enumerate(order)} for order in TILES)
NX, NY, NZ = 4, 4, 8
AXES = (("z", "x", "y"), ("x", "y", "z"), ("y", "z", "x"))
TILES_OF = (3, 5, 4)
FIRST_OF = (0, 3, 8)
COUNT = {"x": NX, "y": NY, "z": NZ}


def spot(at):
    part = 0 if at < 4 * FIRST_OF[1] else 1 if at < 4 * FIRST_OF[2] else 2
    inside = at - 4 * FIRST_OF[part]
    return part, inside // TILES_OF[part], inside % TILES_OF[part]


def chains_of(n):
    return ((1, 0, n // 2), (-1, 1, n // 2), (1, 1, n // 2 - 1), (-1, 0, n // 2 - 1))


def edge_kernel(
    feats_ref, cotan_ref, source_ref, target_ref, angle_ref, w0_hbm, w1_hbm, w2_hbm,
    nodes_out, tiles_out,
    w0_ref, w1_ref, w2_ref, tab_ref, x_s, du_s, trig_s, oh_s, node_ref,
    xt_s, d_s, part0, part1, part2, r10, r11, r12, s20, s21, s22, r20, r21, r22, s30, s31, s32, r30, r31, r32,
    gathered, result, node_in,
    load_sem, share_send, share_recv, send1, recv1, send2, recv2, send3, recv3, all_send, all_recv, node_send, node_recv,
    halo_send, halo_recv,
):
    dp = lax.axis_index("dp")
    graph = lax.axis_index("graph")
    core, x = dp % 2, dp // 2
    y, z = graph % NY, graph // NY
    place = {"x": x, "y": y, "z": z}

    def moved(axis, offset):
        n = COUNT[axis]
        to = (place[axis] + offset + n) % n
        if axis == "x":
            return {"dp": to * 2 + core, "graph": graph}
        if axis == "y":
            return {"dp": dp, "graph": z * NY + to}
        return {"dp": dp, "graph": to * NY + y}

    sibling = {"dp": x * 2 + (1 - core), "graph": graph}
    graphs = NY * NZ
    before = {"dp": dp, "graph": (graph + graphs - 1) % graphs}
    after = {"dp": dp, "graph": (graph + 1) % graphs}
    peers = [{"dp": (dp + o) % 8, "graph": graph} for o in range(1, 8)]
    peers += [moved("y", o) for o in range(1, NY)] + [moved("z", o) for o in range(1, NZ)] + [before, after]

    loads = [
        pltpu.make_async_copy(src, dst, load_sem.at[k])
        for k, (src, dst) in enumerate(((w0_hbm, w0_ref), (w1_hbm, w1_ref), (w2_hbm, w2_ref)))
    ]
    for load in loads:
        load.start()
    feats, cotan = feats_ref[...].astype(F32), cotan_ref[...].astype(F32)
    tab_ref[pl.ds(0, 16)] = jnp.concatenate([feats[:8], cotan[:8]], 0).astype(BF16)
    tab_ref[pl.ds(16, 16)] = jnp.concatenate([feats[8:], cotan[8:]], 0).astype(BF16)
    barrier = pltpu.get_barrier_semaphore()
    for peer in peers:
        pl.semaphore_signal(barrier, inc=1, device_id=peer, device_id_type=MESH)
    pl.semaphore_wait(barrier, len(peers))

    def remote(src, dst, send, recv, device):
        return pltpu.make_async_remote_copy(
            src_ref=src, dst_ref=dst, send_sem=send, recv_sem=recv, device_id=device, device_id_type=MESH
        )

    node_up = remote(node_ref.at[pl.ds(0, 8)], node_in.at[1], node_send.at[0], node_recv.at[0], before)
    node_down = remote(node_ref.at[pl.ds(24, 8)], node_in.at[0], node_send.at[1], node_recv.at[1], after)

    def own_half(kind, lo, hi, half):
        if kind == 0:
            return xt_s.at[pl.ds(lo, hi - lo), :, pl.ds(half * PADDED, PADDED)]
        return d_s.at[pl.ds(lo, hi - lo), pl.ds(half * PADDED, PADDED), :]

    def share_copy(k, span):
        return remote(own_half(*span, 0), own_half(*span, 1), share_send.at[k], share_recv.at[k], sibling)

    stage1 = (part0, part1, part2)
    rings1 = (r10, r11, r12)
    stage2 = (s20, s21, s22)
    rings2 = (r20, r21, r22)
    stage3 = (s30, s31, s32)
    slots3 = (r30, r31, r32)

    def slot_of(n, chain, step):
        return sum(c[2] for c in chains_of(n)[:chain]) + step

    def ring_copy(part, stage, chain, step):
        axis = AXES[part][stage]
        n = COUNT[axis]
        way, half, steps = chains_of(n)[chain]
        source, ring = ((stage1, rings1), (stage2, rings2))[stage]
        sends, recvs = ((send1, recv1), (send2, recv2))[stage]
        deep = source[part].shape[1] // 2
        slot = slot_of(n, chain, step)
        if step == 0:
            block = (place[axis] + way * steps + n) % n
            src = source[part].at[block, pl.ds(half * deep, deep)]
        else:
            src = ring[part].at[slot - 1]
        return remote(src, ring[part].at[slot], sends.at[part, slot], recvs.at[part, slot], moved(axis, way))

    def begin(part, stage):
        for chain in range(4):
            ring_copy(part, stage, chain, 0).start()

    def advance(part, stage, step):
        axis = AXES[part][stage]
        n = COUNT[axis]
        source, ring = ((stage1, rings1), (stage2, rings2))[stage]
        deep = source[part].shape[1] // 2
        for chain, (way, half, steps) in enumerate(chains_of(n)):
            if step < steps:
                slot = slot_of(n, chain, step)
                ring_copy(part, stage, chain, step - 1).wait_recv()
                block = (place[axis] + way * (steps - step) + n) % n
                ring[part][slot - 1] = ring[part][slot - 1] + source[part][block, pl.ds(half * deep, deep)]
                ring_copy(part, stage, chain, step).start()

    def finish(part, stage, out):
        axis = AXES[part][stage]
        n = COUNT[axis]
        source, ring = ((stage1, rings1), (stage2, rings2))[stage]
        deep = source[part].shape[1] // 2
        for half in range(2):
            arrived = []
            for chain, (way, h, steps) in enumerate(chains_of(n)):
                if h == half:
                    ring_copy(part, stage, chain, steps - 1).wait_recv()
                    arrived.append(ring[part][slot_of(n, chain, steps - 1)])
            out[pl.ds(half * deep, deep)] = source[part][place[axis], pl.ds(half * deep, deep)] + arrived[0] + arrived[1]

    def sent(part, stage):
        for chain, (way, half, steps) in enumerate(chains_of(COUNT[AXES[part][stage]])):
            for step in range(steps):
                ring_copy(part, stage, chain, step).wait_send()

    def last_copy(part, offset):
        axis = AXES[part][2]
        n = COUNT[axis]
        return remote(
            stage3[part].at[(place[axis] + offset) % n], slots3[part].at[offset - 1],
            send3.at[part, offset - 1], recv3.at[part, offset - 1], moved(axis, offset),
        )

    def last_begin(part):
        for offset in range(1, COUNT[AXES[part][2]]):
            last_copy(part, offset).start()

    def all_copy(part, offset):
        mine = gathered.at[dp, pl.ds(FIRST_OF[part], TILES_OF[part])]
        return remote(
            mine, mine, all_send.at[part, offset - 1], all_recv.at[part, offset - 1],
            {"dp": (dp + offset) % 8, "graph": graph},
        )

    def last_end(part):
        axis = AXES[part][2]
        whole = stage3[part][place[axis]]
        for offset in range(1, COUNT[axis]):
            last_copy(part, offset).wait_recv()
            whole = whole + slots3[part][offset - 1]
        gathered[dp, pl.ds(FIRST_OF[part], TILES_OF[part])] = whole
        for offset in range(1, 8):
            all_copy(part, offset).start()

    def put(which, tile, row_y, v):
        at = PLACE[which][tile]
        part, px, pk = spot(at)
        if part == 0:
            part0[:, px, row_y, pk] = v
        elif part == 1:
            part1[px, row_y, :, pk] = v
        else:
            part2[row_y, :, px, pk] = v

    def pair(block, width):
        return jnp.concatenate([d_s[block + k] for k in range(width)], axis=1)

    def factor(block, count):
        return xt_s[pl.ds(block, count)].reshape(count * LANES, 2 * PADDED)

    def put_aligned(v, first_blocks):
        shaped = v.reshape(NZ, NY * 3, 8, v.shape[1])
        for w, b in enumerate(first_blocks):
            for row_y in range(NY):
                for i in range(3):
                    put(0, (1, i, b), row_y, shaped[:, row_y * 3 + i, :, w * LANES : (w + 1) * LANES])

    def put_shifted(which, matrix, tiles, shard, v, first_blocks):
        result[:, pl.ds(0, NY * shard), pl.ds(0, v.shape[1])] = v.reshape(NZ, NY * shard, v.shape[1])
        for w, b in enumerate(first_blocks):
            for row_y in range(NY):
                for i in range(tiles):
                    put(which, (matrix, i, b), row_y, result[:, pl.ds(row_y * shard + i * 8, 8), cols(w)])

    def two_blocks(which, at, width):
        dp_, dn_ = pair(AT_P2 + at, width), pair(AT_N2 + at, width)
        rp, rn = factor(AT_P2, TWO), factor(AT_N2, TWO)
        put_shifted(which, 2, 3, 20, dot(rp, dp_) + dot(rn, dn_), range(at, at + width))
        put_shifted(which, 2, 3, 20, dot(rp, dn_) - dot(rn, dp_), range(TWO + at, TWO + at + width))


    halo_down = remote(tab_ref.at[pl.ds(16, 16)], tab_ref.at[pl.ds(32, 16)], halo_send.at[0], halo_recv.at[0], after)
    halo_up = remote(tab_ref.at[pl.ds(0, 16)], tab_ref.at[pl.ds(48, 16)], halo_send.at[1], halo_recv.at[1], before)
    halo_down.start()
    halo_up.start()

    first_atom = graph * 16 - 8

    def table_row(atoms, shift):
        local = atoms - first_atom
        block = local >> 3
        base = jnp.where(block == 0, 32, jnp.where(block == 1, 0, jnp.where(block == 2, 16, 48)))
        return (base + (local & 7) + shift).astype(F32)

    row = lax.broadcasted_iota(jnp.int32, (8, EDGES), 0)
    phases = jnp.broadcast_to(angle_ref[...], (8, EDGES))
    phases = jnp.where(row < 2, phases, 2.0 * phases)
    ends = jnp.where(row == 4, table_row(source_ref[...], 0), table_row(target_ref[...], 8))
    rows = jnp.where(row >= 4, ends, jnp.where((row & 1) == 0, jnp.cos(phases), jnp.sin(phases)))
    parts = jnp.concatenate(list(split3(rows)), axis=0)
    pick_row = lax.broadcasted_iota(jnp.int32, (24, 6 * LANES), 0)
    pick_col = lax.broadcasted_iota(jnp.int32, (24, 6 * LANES), 1)
    chosen = jnp.where(pick_row % 8 == pick_col // LANES, 1.0, 0.0).astype(BF16)
    spread = dot_first(parts, chosen)
    for k in range(4):
        trig_s[k] = spread[:, k * LANES : (k + 1) * LANES]
    lane = lax.broadcasted_iota(jnp.int32, (EDGES, LANES), 1).astype(F32)
    for k in range(2):
        oh_s[k] = jnp.where(spread[:, (4 + k) * LANES : (5 + k) * LANES] == lane, 1.0, 0.0).astype(BF16)
    depth = tab_ref.shape[0]
    oh_src = oh_s[0, :, :depth]
    oh_dst = oh_s[1, :, :depth]

    xt_s[:, :, EDGES:PADDED] = jnp.zeros((BLOCKS, LANES, PADDED - EDGES), BF16)
    d_s[:, EDGES:PADDED, :] = jnp.zeros((BLOCKS, PADDED - EDGES, LANES), BF16)
    result[...] = jnp.zeros_like(result)
    halo_down.wait_recv()
    halo_up.wait_recv()

    def keep_x(block, width, v):
        x_s[:, cols(block, width)] = v
        for w in range(width):
            xt_s[block + w, :, :EDGES] = v[:, w * LANES : (w + 1) * LANES].T

    def rotated(onehot, c, s, plus, minus, width):
        a = dot(onehot, tab_ref[:, cols(plus, width)])
        b = dot(onehot, tab_ref[:, cols(minus, width)])
        return c * a - s * b, s * a + c * b

    for at, width in chunks(ZERO):
        keep_x(at, width, dot(oh_src, tab_ref[:, cols(at, width)]).astype(BF16))
    for m, (count, plus, minus) in enumerate(((ONE, AT_P1, AT_N1), (TWO, AT_P2, AT_N2))):
        for at, width in chunks(count):
            c, s = wide(trig_s[2 * m], width), wide(trig_s[2 * m + 1], width)
            p, n = rotated(oh_src, c, s, plus + at, minus + at, width)
            keep_x(plus + at, width, p.astype(BF16))
            keep_x(minus + at, width, n.astype(BF16))


    def share(kind):
        @pl.when(core == 0)
        def _():
            for k, span in enumerate(SHARES[1]):
                if span[0] == kind:
                    share_copy(k, span).start()

        @pl.when(core == 1)
        def _():
            for k, span in enumerate(SHARES[0]):
                if span[0] == kind:
                    share_copy(k, span).start()

    share(0)
    for load in loads:
        load.wait()
    total = jnp.zeros((EDGES, LANES), F32)
    first = None
    for at, width in chunks(ZERO):
        out = dot(x_s[:, cols(0, ZERO)], w0_ref[:, cols(at, width)])
        if at == 0:
            first = out[:, :LANES]
        up = dot(oh_dst, tab_ref[:, cols(at, width)])
        du_s[:, cols(at, width)] = up
        total = total + folded(up * out, width)
    for m, (count, plus, minus, w_ref) in enumerate(((ONE, AT_P1, AT_N1, w1_ref), (TWO, AT_P2, AT_N2, w2_ref))):
        for at, width in chunks(count):
            c, s = wide(trig_s[2 * m], width), wide(trig_s[2 * m + 1], width)
            up_p, up_n = rotated(oh_dst, c, s, plus + at, minus + at, width)
            du_s[:, cols(plus + at, width)] = up_p
            du_s[:, cols(minus + at, width)] = up_n
            xp, xn = x_s[:, cols(plus, count)], x_s[:, cols(minus, count)]
            left, right = w_ref[:, cols(at, width)], w_ref[:, cols(count + at, width)]
            out_p = dot(xp, left) - dot(xn, right)
            out_n = dot(xp, right) + dot(xn, left)
            total = total + folded(up_p * out_p + up_n * out_n, width)

    size = LANES // HEADS
    head_r = lax.broadcasted_iota(jnp.int32, (LANES, LANES), 0) // size
    head_c = lax.broadcasted_iota(jnp.int32, (LANES, LANES), 1) // size
    same = jnp.where(head_r == head_c, 1.0, 0.0).astype(BF16)

    def head_sum(v):
        high, middle, low = split3(v)
        return dot(low, same) + dot(middle, same) + dot(high, same)

    scale = 1.0 / (float(size) ** 0.5)
    gate = jax.nn.sigmoid(head_sum(first) * scale)
    dlogit = head_sum(total) * gate * (1.0 - gate) * scale
    for block in range(BLOCKS):
        v = du_s[:, cols(block)] * gate
        if block == 0:
            v = v + dlogit
        d_s[block, :EDGES, :] = v.astype(BF16)

    share(1)


    @pl.when(core == 0)
    def _():
        for k, span in enumerate(SHARES[0]):
            share_copy(k, span).wait_recv()
        for j in range(3):
            dp_, dn_ = pair(AT_P1 + 2 * j, 2), pair(AT_N1 + 2 * j, 2)
            rp, rn = factor(AT_P1, ONE), factor(AT_N1, ONE)
            put_aligned(dot(rp, dp_) + dot(rn, dn_), (2 * j, 2 * j + 1))
            put_aligned(dot(rp, dn_) - dot(rn, dp_), (6 + 2 * j, 7 + 2 * j))
            if j == 0:
                begin(0, 0)
        begin(1, 0)
        two_blocks(0, 0, 2)
        begin(2, 0)
        for k, span in enumerate(SHARES[1]):
            share_copy(k, span).wait_send()

    @pl.when(core == 1)
    def _():
        for k, span in enumerate(SHARES[1]):
            share_copy(k, span).wait_recv()
        blank = jnp.zeros((NZ, 8, LANES), F32)
        for row_y in range(NY):
            for k in (2, 3):
                part2[row_y, :, 3, k] = blank
        for at, width in chunks(ZERO):
            put_shifted(1, 0, 4, 28, dot(factor(AT_Z, ZERO), pair(AT_Z + at, width)), range(at, at + width))
            if at == 2:
                begin(0, 0)
        two_blocks(1, 2, 2)
        begin(1, 0)
        two_blocks(1, 4, 1)
        begin(2, 0)
        for k, span in enumerate(SHARES[0]):
            share_copy(k, span).wait_send()

    atoms = node_ref.shape[0]
    atom = lax.broadcasted_iota(jnp.int32, (atoms, EDGES), 0)
    table_row = jnp.where(atom < 8, atom + 32, jnp.where(atom < 16, atom - 8, jnp.where(atom < 24, atom, atom + 24)))
    oh_rows = jnp.where(table_row.astype(F32) == rows[4:5, :], 1.0, 0.0).astype(BF16)

    def scatter(block, width, v):
        high, low = split2(v)
        node_ref[:, cols(block, width)] = dot(oh_rows, high) + dot(oh_rows, low)

    def dconv(block, count):
        return jnp.concatenate([d_s[block + k, :EDGES, :] for k in range(count)], axis=1)

    dz = dconv(AT_Z, ZERO)
    for at, width in chunks(ZERO):
        scatter(at, width, dot_t(dz, w0_ref[cols(at, width), :]))
    for m, (count, plus, minus, w_ref) in enumerate(((ONE, AT_P1, AT_N1, w1_ref), (TWO, AT_P2, AT_N2, w2_ref))):
        gp, gn = dconv(plus, count), dconv(minus, count)
        for at, width in chunks(count):
            c, s = wide(trig_s[2 * m], width), wide(trig_s[2 * m + 1], width)
            left, right = w_ref[cols(at, width), cols(0, count)], w_ref[cols(at, width), cols(count, count)]
            back_p = dot_t(gp, left) + dot_t(gn, right)
            back_n = dot_t(gn, left) - dot_t(gp, right)
            scatter(plus + at, width, c * back_p + s * back_n)
            scatter(minus + at, width, c * back_n - s * back_p)


    node_up.start()
    node_down.start()

    for part in (1, 2):
        advance(part, 0, 1)
    advance(0, 0, 1)
    advance(0, 0, 2)
    node_up.wait()
    node_down.wait()
    nodes_out[pl.ds(0, 8)] = (node_ref[pl.ds(8, 8)] + node_in[0]).astype(BF16)
    nodes_out[pl.ds(8, 8)] = (node_ref[pl.ds(16, 8)] + node_in[1]).astype(BF16)
    advance(0, 0, 3)
    finish(1, 0, s21)
    begin(1, 1)
    finish(2, 0, s22)
    begin(2, 1)
    finish(0, 0, s20)
    begin(0, 1)
    advance(1, 1, 1)
    advance(2, 1, 1)
    advance(0, 1, 1)
    finish(1, 1, s31)
    last_begin(1)
    advance(2, 1, 2)
    finish(0, 1, s30)
    last_begin(0)
    advance(2, 1, 3)
    last_end(0)
    last_end(1)
    finish(2, 1, s32)
    last_begin(2)
    last_end(2)
    for part in range(3):
        for stage in range(2):
            sent(part, stage)
        for offset in range(1, COUNT[AXES[part][2]]):
            last_copy(part, offset).wait_send()
    for part in range(3):
        for offset in range(1, 8):
            all_copy(part, offset).wait_recv()
    tiles_out[...] = gathered[...] * 0.125
    for part in range(3):
        for offset in range(1, 8):
            all_copy(part, offset).wait_send()
    halo_down.wait_send()
    halo_up.wait_send()


def place_kernel(tiles_ref, nodes_ref, nodes_out, zero_out, one_out, two_out):
    nodes_out[...] = nodes_ref[...]
    outs = (zero_out, one_out, two_out)
    for which in range(2):
        for at, (matrix, i, b) in enumerate(TILES[which]):
            part, px, pk = spot(at)
            out = outs[matrix]
            rows = min(8, out.shape[0] - 8 * i)
            out[pl.ds(8 * i, rows), cols(b)] = tiles_ref[px * 2 + which, FIRST_OF[part] + pk, pl.ds(0, rows)]


def shards(node_feats, node_cotan, source, target, angle, w_zero, w_one, w_two):
    width = node_feats.shape[2]
    vmem = pl.BlockSpec(memory_space=pltpu.VMEM)
    hbm = pl.BlockSpec(memory_space=pl.ANY)
    dims = [[COUNT[a] for a in axes] for axes in AXES]
    tile = [(k, 8, LANES) for k in TILES_OF]

    def ring(part, stage):
        n = dims[part][stage]
        inner = dims[part][stage + 1 :]
        return pltpu.VMEM((2 * (n - 1), inner[0] // 2, *inner[1:], *tile[part]), F32)

    dma = pltpu.SemaphoreType.DMA
    nodes, tiles = pl.pallas_call(
        edge_kernel,
        out_shape=(
            jax.ShapeDtypeStruct((16, width), BF16),
            jax.ShapeDtypeStruct((8, 12, 8, LANES), F32),
        ),
        in_specs=[vmem] * 5 + [hbm] * 3,
        out_specs=(vmem,) * 2,
        scratch_shapes=[
            pltpu.VMEM(w_zero.shape, BF16),
            pltpu.VMEM(w_one.shape, BF16),
            pltpu.VMEM(w_two.shape, BF16),
            pltpu.VMEM((64, width), BF16),
            pltpu.VMEM((EDGES, width), BF16),
            pltpu.VMEM((EDGES, width), F32),
            pltpu.VMEM((4, EDGES, LANES), F32),
            pltpu.VMEM((2, EDGES, LANES), BF16),
            pltpu.VMEM((32, width), F32),
            pltpu.VMEM((BLOCKS, LANES, 2 * PADDED), BF16),
            pltpu.VMEM((BLOCKS, 2 * PADDED, LANES), BF16),
            *[pltpu.VMEM((*dims[p], *tile[p]), F32) for p in range(3)],
            *[ring(p, 0) for p in range(3)],
            *[pltpu.VMEM((*dims[p][1:], *tile[p]), F32) for p in range(3)],
            *[ring(p, 1) for p in range(3)],
            *[pltpu.VMEM((dims[p][2], *tile[p]), F32) for p in range(3)],
            *[pltpu.VMEM((dims[p][2] - 1, *tile[p]), F32) for p in range(3)],
            pltpu.VMEM((8, 12, 8, LANES), F32),
            pltpu.VMEM((NZ, 120, 2 * LANES), F32),
            pltpu.VMEM((2, 8, width), F32),
            dma((3,)), dma((5,)), dma((5,)),
            dma((3, 14)), dma((3, 14)), dma((3, 14)), dma((3, 14)), dma((3, 7)), dma((3, 7)),
            dma((3, 7)), dma((3, 7)), dma((2,)), dma((2,)), dma((2,)), dma((2,)),
        ],
        compiler_params=pltpu.CompilerParams(
            vmem_limit_bytes=VMEM_LIMIT, collective_id=0, has_side_effects=True
        ),
        name="edge_gradients",
    )(node_feats[0], node_cotan[0], source, target, angle, w_zero, w_one, w_two)
    nodes, zero_g, one_g, two_g = pl.pallas_call(
        place_kernel,
        out_shape=(
            jax.ShapeDtypeStruct((16, width), BF16),
            jax.ShapeDtypeStruct((28, ZERO * LANES), F32),
            jax.ShapeDtypeStruct((24, 2 * ONE * LANES), F32),
            jax.ShapeDtypeStruct((20, 2 * TWO * LANES), F32),
        ),
        in_specs=[vmem] * 2,
        out_specs=(vmem,) * 4,
        name="place_tiles",
    )(tiles, nodes)
    return nodes[None], zero_g, one_g, two_g


def solution(mesh):
    placed = (
        P("dp", "graph", None),
        P("dp", "graph", None),
        P("dp", "graph"),
        P("dp", "graph"),
        P("dp", "graph"),
        P(),
        P(),
        P(),
    )
    return jax.shard_map(
        shards,
        mesh=mesh,
        in_specs=placed,
        out_specs=(P("dp", "graph", None), P("graph", None), P("graph", None), P("graph", None)),
        check_vma=False,
    )
```

time: 105 us -> 83 us (0.79)
  local copies, waits for them, and re-layouts: 11.9 us -> 0 us
  starting transfers between devices: 9.02 us -> 0 us
  other arithmetic: 2.22 us -> 0 us
  Pallas kernels: 80.9 us -> 82.3 us
    unnamed x11 -> x0, local copies, waits for them, and re-layouts: 10.4 us -> none
    ppermute x2 -> x0, starting transfers between devices: 9.02 us -> none  [the longest x1 6.82 us: shards(): lax.ppermute(own_low, 'graph', [((i + 1) % graphs, i) for i in range(grap...]
    pallas_call x2, Pallas kernels: 80.9 us -> 82.3 us  [the longest x1 80.5 us: shards(): pl.pallas_call(edge_kernel, out_shape=(jax.ShapeDtypeStruct((16, width),...]
  transfers between devices with their start and end apart: 2 -> 0, of which waited for: 0 -> 0; matrix products, arithmetic and copies ran while one was open for 6% -> 0% of each run, Pallas kernels for 0% -> 0%
where the time goes in v2:
time: 83 us; the launch traced here: 82.9 us
  Pallas kernels  82.3 us (99%)
    pallas_call x1, Pallas kernels, shards(): pl.pallas_call(edge_kernel, out_shape=(jax.ShapeDtypeStruct((16, width),...  80.5 us
    pallas_call x1, Pallas kernels, shards(): pl.pallas_call(place_kernel, out_shape=(jax.ShapeDtypeStruct((16, width),...  1.8 us

profile of v2, /device:TPU:1, one launch (start us, length us, event | category | flops | bytes accessed | tf_op | source)
XLA Modules:
  0.0 82.9 jit_solution(10336256743616998934)
XLA Ops:
  0.6 80.5 %edge_gradients.1 = (bf16[16,3712]{1,0:T(8,128)(2,1)}, f32[8,12,8,128]{3,2,1,0:T(8,128)}) custom-call(bf16[16,3712]{1,0:T(8,128)(2,1)} %bitcast.3, bf16[16,3712]{1,0:T(8,128)(2,1)} %bitcast.4, s32[1,320]{1,0:T(1,128)} %source_ref.1, s32[1,320]{1,0:T(1,128)} %target_ref.1, f32[1,320]{1,0:T(1,128)} %angle_ref.1, bf16[896,896]{1,0:T(8,128)(2,1)} %w0_hbm.1, ...), custom_call_target="tpu_custom_call" | custom-call | tf_op jit(solution)/shard_map/edge_gradients/pallas_call | solution.py:530
  81.1 1.8 %place_tiles.1 = (bf16[16,3712]{1,0:T(8,128)(2,1)}, f32[28,896]{1,0:T(8,128)}, f32[24,1536]{1,0:T(8,128)}, f32[20,1280]{1,0:T(8,128)}) custom-call(f32[8,12,8,128]{3,2,1,0:T(8,128)} %get-tuple-element.10.tiles_ref, bf16[16,3712]{1,0:T(8,128)(2,1)} %get-tuple-element.11.nodes_ref), custom_call_target="tpu_custom_call" | custom-call | tf_op jit(solution)/shard_map/place_tiles/pallas_call | solution.py:568

commit v3 on v2

--- a/solution.py
+++ b/solution.py
@@ -74,9 +74,9 @@
 )
 PLACE = tuple({tile: at for at, tile in enumerate(order)} for order in TILES)
 NX, NY, NZ = 4, 4, 8
-AXES = (("z", "x", "y"), ("x", "y", "z"), ("y", "z", "x"))
-TILES_OF = (3, 5, 4)
-FIRST_OF = (0, 3, 8)
+AXES = (("z", "x", "y"), ("x", "y", "z"), ("y", "x", "z"))
+TILES_OF = (3, 4, 5)
+FIRST_OF = (0, TILES_OF[0], TILES_OF[0] + TILES_OF[1])
 COUNT = {"x": NX, "y": NY, "z": NZ}
 
 
@@ -95,7 +95,7 @@
     nodes_out, tiles_out,
     w0_ref, w1_ref, w2_ref, tab_ref, x_s, du_s, trig_s, oh_s, node_ref,
     xt_s, d_s, part0, part1, part2, r10, r11, r12, s20, s21, s22, r20, r21, r22, s30, s31, s32, r30, r31, r32,
-    gathered, result, node_in,
+    o0, o1, o2, i0, i1, i2, gathered, result, node_in,
     load_sem, share_send, share_recv, send1, recv1, send2, recv2, send3, recv3, all_send, all_recv, node_send, node_recv,
     halo_send, halo_recv,
 ):
@@ -121,6 +121,9 @@
     peers = [{"dp": (dp + o) % 8, "graph": graph} for o in range(1, 8)]
     peers += [moved("y", o) for o in range(1, NY)] + [moved("z", o) for o in range(1, NZ)] + [before, after]
 
+    barrier = pltpu.get_barrier_semaphore()
+    for peer in peers:
+        pl.semaphore_signal(barrier, inc=1, device_id=peer, device_id_type=MESH)
     loads = [
         pltpu.make_async_copy(src, dst, load_sem.at[k])
         for k, (src, dst) in enumerate(((w0_hbm, w0_ref), (w1_hbm, w1_ref), (w2_hbm, w2_ref)))
@@ -130,11 +133,6 @@
     feats, cotan = feats_ref[...].astype(F32), cotan_ref[...].astype(F32)
     tab_ref[pl.ds(0, 16)] = jnp.concatenate([feats[:8], cotan[:8]], 0).astype(BF16)
     tab_ref[pl.ds(16, 16)] = jnp.concatenate([feats[8:], cotan[8:]], 0).astype(BF16)
-    barrier = pltpu.get_barrier_semaphore()
-    for peer in peers:
-        pl.semaphore_signal(barrier, inc=1, device_id=peer, device_id_type=MESH)
-    pl.semaphore_wait(barrier, len(peers))
-
     def remote(src, dst, send, recv, device):
         return pltpu.make_async_remote_copy(
             src_ref=src, dst_ref=dst, send_sem=send, recv_sem=recv, device_id=device, device_id_type=MESH
@@ -157,6 +155,8 @@
     rings2 = (r20, r21, r22)
     stage3 = (s30, s31, s32)
     slots3 = (r30, r31, r32)
+
+    outs16, ins16 = (o0, o1, o2), (i0, i1, i2)
 
     def slot_of(n, chain, step):
         return sum(c[2] for c in chains_of(n)[:chain]) + step
@@ -169,6 +169,11 @@
         sends, recvs = ((send1, recv1), (send2, recv2))[stage]
         deep = source[part].shape[1] // 2
         slot = slot_of(n, chain, step)
+        if step == 0 and stage == 0:
+            return remote(
+                outs16[part].at[chain], ins16[part].at[chain],
+                sends.at[part, slot], recvs.at[part, slot], moved(axis, way),
+            )
         if step == 0:
             block = (place[axis] + way * steps + n) % n
             src = source[part].at[block, pl.ds(half * deep, deep)]
@@ -177,8 +182,22 @@
         return remote(src, ring[part].at[slot], sends.at[part, slot], recvs.at[part, slot], moved(axis, way))
 
     def begin(part, stage):
-        for chain in range(4):
+        axis = AXES[part][stage]
+        n = COUNT[axis]
+        for chain, (way, half, steps) in enumerate(chains_of(n)):
+            if stage == 0:
+                deep = stage1[part].shape[1] // 2
+                block = (place[axis] + way * steps + n) % n
+                v = stage1[part][block, pl.ds(half * deep, deep)]
+                outs16[part][chain] = v.reshape(outs16[part].shape[1:]).astype(BF16)
             ring_copy(part, stage, chain, 0).start()
+
+    def arrival(part, stage, chain, step):
+        n = COUNT[AXES[part][stage]]
+        ring = (rings1, rings2)[stage][part]
+        if stage == 0 and step == 0:
+            return ins16[part][chain].astype(F32).reshape(ring.shape[1:])
+        return ring[slot_of(n, chain, step)]
 
     def advance(part, stage, step):
         axis = AXES[part][stage]
@@ -190,7 +209,7 @@
                 slot = slot_of(n, chain, step)
                 ring_copy(part, stage, chain, step - 1).wait_recv()
                 block = (place[axis] + way * (steps - step) + n) % n
-                ring[part][slot - 1] = ring[part][slot - 1] + source[part][block, pl.ds(half * deep, deep)]
+                ring[part][slot - 1] = arrival(part, stage, chain, step - 1) + source[part][block, pl.ds(half * deep, deep)]
                 ring_copy(part, stage, chain, step).start()
 
     def finish(part, stage, out):
@@ -203,7 +222,7 @@
             for chain, (way, h, steps) in enumerate(chains_of(n)):
                 if h == half:
                     ring_copy(part, stage, chain, steps - 1).wait_recv()
-                    arrived.append(ring[part][slot_of(n, chain, steps - 1)])
+                    arrived.append(arrival(part, stage, chain, steps - 1))
             out[pl.ds(half * deep, deep)] = source[part][place[axis], pl.ds(half * deep, deep)] + arrived[0] + arrived[1]
 
     def sent(part, stage):
@@ -240,6 +259,11 @@
         for offset in range(1, 8):
             all_copy(part, offset).start()
 
+    def ready(had, have):
+        for part in range(3):
+            if had < 4 * (FIRST_OF[part] + TILES_OF[part]) <= have:
+                begin(part, 0)
+
     def put(which, tile, row_y, v):
         at = PLACE[which][tile]
         part, px, pk = spot(at)
@@ -248,7 +272,7 @@
         elif part == 1:
             part1[px, row_y, :, pk] = v
         else:
-            part2[row_y, :, px, pk] = v
+            part2[row_y, px, :, pk] = v
 
     def pair(block, width):
         return jnp.concatenate([d_s[block + k] for k in range(width)], axis=1)
@@ -277,10 +301,20 @@
         put_shifted(which, 2, 3, 20, dot(rp, dn_) - dot(rn, dp_), range(TWO + at, TWO + at + width))
 
 
-    halo_down = remote(tab_ref.at[pl.ds(16, 16)], tab_ref.at[pl.ds(32, 16)], halo_send.at[0], halo_recv.at[0], after)
-    halo_up = remote(tab_ref.at[pl.ds(0, 16)], tab_ref.at[pl.ds(48, 16)], halo_send.at[1], halo_recv.at[1], before)
-    halo_down.start()
-    halo_up.start()
+    orders = ((0, AT_P1), (AT_P1, AT_P2), (AT_P2, BLOCKS))
+
+    def halo_copies(k):
+        span = pl.ds(orders[k][0] * LANES, (orders[k][1] - orders[k][0]) * LANES)
+        return (
+            remote(
+                tab_ref.at[pl.ds(16, 16), span], tab_ref.at[pl.ds(32, 16), span],
+                halo_send.at[k, 0], halo_recv.at[k, 0], after,
+            ),
+            remote(
+                tab_ref.at[pl.ds(0, 16), span], tab_ref.at[pl.ds(48, 16), span],
+                halo_send.at[k, 1], halo_recv.at[k, 1], before,
+            ),
+        )
 
     first_atom = graph * 16 - 8
 
@@ -309,11 +343,14 @@
     oh_src = oh_s[0, :, :depth]
     oh_dst = oh_s[1, :, :depth]
 
+    pl.semaphore_wait(barrier, len(peers))
+
+    for k in range(3):
+        for copy in halo_copies(k):
+            copy.start()
     xt_s[:, :, EDGES:PADDED] = jnp.zeros((BLOCKS, LANES, PADDED - EDGES), BF16)
     d_s[:, EDGES:PADDED, :] = jnp.zeros((BLOCKS, PADDED - EDGES, LANES), BF16)
     result[...] = jnp.zeros_like(result)
-    halo_down.wait_recv()
-    halo_up.wait_recv()
 
     def keep_x(block, width, v):
         x_s[:, cols(block, width)] = v
@@ -325,9 +362,13 @@
         b = dot(onehot, tab_ref[:, cols(minus, width)])
         return c * a - s * b, s * a + c * b
 
+    for copy in halo_copies(0):
+        copy.wait_recv()
     for at, width in chunks(ZERO):
         keep_x(at, width, dot(oh_src, tab_ref[:, cols(at, width)]).astype(BF16))
     for m, (count, plus, minus) in enumerate(((ONE, AT_P1, AT_N1), (TWO, AT_P2, AT_N2))):
+        for copy in halo_copies(1 + m):
+            copy.wait_recv()
         for at, width in chunks(count):
             c, s = wide(trig_s[2 * m], width), wide(trig_s[2 * m + 1], width)
             p, n = rotated(oh_src, c, s, plus + at, minus + at, width)
@@ -335,20 +376,15 @@
             keep_x(minus + at, width, n.astype(BF16))
 
 
-    def share(kind):
-        @pl.when(core == 0)
-        def _():
-            for k, span in enumerate(SHARES[1]):
-                if span[0] == kind:
-                    share_copy(k, span).start()
-
-        @pl.when(core == 1)
-        def _():
-            for k, span in enumerate(SHARES[0]):
-                if span[0] == kind:
-                    share_copy(k, span).start()
-
-    share(0)
+    def share(kind, lo, hi):
+        for other in range(2):
+            @pl.when(core == 1 - other)
+            def _(other=other):
+                for k, span in enumerate(SHARES[other]):
+                    if span[0] == kind and lo < span[2] <= hi:
+                        share_copy(k, span).start()
+
+    share(0, 0, BLOCKS)
     for load in loads:
         load.wait()
     total = jnp.zeros((EDGES, LANES), F32)
@@ -389,10 +425,37 @@
         if block == 0:
             v = v + dlogit
         d_s[block, :EDGES, :] = v.astype(BF16)
-
-    share(1)
-
-
+        if any(block + 1 == span[2] for spans in SHARES for span in spans if span[0]):
+            share(1, block, block + 1)
+
+
+    atoms = node_ref.shape[0]
+    atom = lax.broadcasted_iota(jnp.int32, (atoms, EDGES), 0)
+    table_row = jnp.where(atom < 8, atom + 32, jnp.where(atom < 16, atom - 8, jnp.where(atom < 24, atom, atom + 24)))
+    oh_rows = jnp.where(table_row.astype(F32) == rows[4:5, :], 1.0, 0.0).astype(BF16)
+
+    def scatter(block, width, v):
+        high, low = split2(v)
+        node_ref[:, cols(block, width)] = dot(oh_rows, high) + dot(oh_rows, low)
+
+    def dconv(block, count):
+        return jnp.concatenate([d_s[block + k, :EDGES, :] for k in range(count)], axis=1)
+
+    def back(m, picked):
+        count, plus, minus, w_ref = ((ONE, AT_P1, AT_N1, w1_ref), (TWO, AT_P2, AT_N2, w2_ref))[m]
+        gp, gn = dconv(plus, count), dconv(minus, count)
+        for at, width in chunks(count)[picked]:
+            c, s = wide(trig_s[2 * m], width), wide(trig_s[2 * m + 1], width)
+            left, right = w_ref[cols(at, width), cols(0, count)], w_ref[cols(at, width), cols(count, count)]
+            back_p = dot_t(gp, left) + dot_t(gn, right)
+            back_n = dot_t(gn, left) - dot_t(gp, right)
+            scatter(plus + at, width, c * back_p + s * back_n)
+            scatter(minus + at, width, c * back_n - s * back_p)
+
+
+    dz = dconv(AT_Z, ZERO)
+    for at, width in chunks(ZERO):
+        scatter(at, width, dot_t(dz, w0_ref[cols(at, width), :]))
     @pl.when(core == 0)
     def _():
         for k, span in enumerate(SHARES[0]):
@@ -402,11 +465,9 @@
             rp, rn = factor(AT_P1, ONE), factor(AT_N1, ONE)
             put_aligned(dot(rp, dp_) + dot(rn, dn_), (2 * j, 2 * j + 1))
             put_aligned(dot(rp, dn_) - dot(rn, dp_), (6 + 2 * j, 7 + 2 * j))
-            if j == 0:
-                begin(0, 0)
-        begin(1, 0)
+            ready(12 * j, 12 * j + 12)
         two_blocks(0, 0, 2)
-        begin(2, 0)
+        ready(36, 48)
         for k, span in enumerate(SHARES[1]):
             share_copy(k, span).wait_send()
 
@@ -416,76 +477,49 @@
             share_copy(k, span).wait_recv()
         blank = jnp.zeros((NZ, 8, LANES), F32)
         for row_y in range(NY):
-            for k in (2, 3):
-                part2[row_y, :, 3, k] = blank
+            for at in (46, 47):
+                part2[row_y, spot(at)[1], :, spot(at)[2]] = blank
         for at, width in chunks(ZERO):
             put_shifted(1, 0, 4, 28, dot(factor(AT_Z, ZERO), pair(AT_Z + at, width)), range(at, at + width))
-            if at == 2:
-                begin(0, 0)
+            ready(4 * at, 4 * (at + width))
         two_blocks(1, 2, 2)
-        begin(1, 0)
         two_blocks(1, 4, 1)
-        begin(2, 0)
+        ready(28, 48)
         for k, span in enumerate(SHARES[0]):
             share_copy(k, span).wait_send()
 
-    atoms = node_ref.shape[0]
-    atom = lax.broadcasted_iota(jnp.int32, (atoms, EDGES), 0)
-    table_row = jnp.where(atom < 8, atom + 32, jnp.where(atom < 16, atom - 8, jnp.where(atom < 24, atom, atom + 24)))
-    oh_rows = jnp.where(table_row.astype(F32) == rows[4:5, :], 1.0, 0.0).astype(BF16)
-
-    def scatter(block, width, v):
-        high, low = split2(v)
-        node_ref[:, cols(block, width)] = dot(oh_rows, high) + dot(oh_rows, low)
-
-    def dconv(block, count):
-        return jnp.concatenate([d_s[block + k, :EDGES, :] for k in range(count)], axis=1)
-
-    dz = dconv(AT_Z, ZERO)
-    for at, width in chunks(ZERO):
-        scatter(at, width, dot_t(dz, w0_ref[cols(at, width), :]))
-    for m, (count, plus, minus, w_ref) in enumerate(((ONE, AT_P1, AT_N1, w1_ref), (TWO, AT_P2, AT_N2, w2_ref))):
-        gp, gn = dconv(plus, count), dconv(minus, count)
-        for at, width in chunks(count):
-            c, s = wide(trig_s[2 * m], width), wide(trig_s[2 * m + 1], width)
-            left, right = w_ref[cols(at, width), cols(0, count)], w_ref[cols(at, width), cols(count, count)]
-            back_p = dot_t(gp, left) + dot_t(gn, right)
-            back_n = dot_t(gn, left) - dot_t(gp, right)
-            scatter(plus + at, width, c * back_p + s * back_n)
-            scatter(minus + at, width, c * back_n - s * back_p)
-
-
+    back(0, slice(0, 1))
+    advance(0, 0, 1)
+    back(0, slice(1, 3))
+    advance(0, 0, 2)
+    advance(1, 0, 1)
+    advance(2, 0, 1)
+    back(1, slice(0, 1))
+    advance(0, 0, 3)
+    back(1, slice(1, 3))
     node_up.start()
     node_down.start()
-
-    for part in (1, 2):
-        advance(part, 0, 1)
-    advance(0, 0, 1)
-    advance(0, 0, 2)
+    finish(0, 0, s20)
+    begin(0, 1)
+    finish(1, 0, s21)
+    begin(1, 1)
+    finish(2, 0, s22)
+    begin(2, 1)
+    advance(0, 1, 1)
+    advance(1, 1, 1)
+    advance(2, 1, 1)
+    finish(0, 1, s30)
+    last_begin(0)
+    finish(1, 1, s31)
+    last_begin(1)
+    finish(2, 1, s32)
+    last_begin(2)
+    last_end(0)
     node_up.wait()
     node_down.wait()
     nodes_out[pl.ds(0, 8)] = (node_ref[pl.ds(8, 8)] + node_in[0]).astype(BF16)
     nodes_out[pl.ds(8, 8)] = (node_ref[pl.ds(16, 8)] + node_in[1]).astype(BF16)
-    advance(0, 0, 3)
-    finish(1, 0, s21)
-    begin(1, 1)
-    finish(2, 0, s22)
-    begin(2, 1)
-    finish(0, 0, s20)
-    begin(0, 1)
-    advance(1, 1, 1)
-    advance(2, 1, 1)
-    advance(0, 1, 1)
-    finish(1, 1, s31)
-    last_begin(1)
-    advance(2, 1, 2)
-    finish(0, 1, s30)
-    last_begin(0)
-    advance(2, 1, 3)
-    last_end(0)
     last_end(1)
-    finish(2, 1, s32)
-    last_begin(2)
     last_end(2)
     for part in range(3):
         for stage in range(2):
@@ -499,8 +533,9 @@
     for part in range(3):
         for offset in range(1, 8):
             all_copy(part, offset).wait_send()
-    halo_down.wait_send()
-    halo_up.wait_send()
+    for k in range(3):
+        for copy in halo_copies(k):
+            copy.wait_send()
 
 
 def place_kernel(tiles_ref, nodes_ref, nodes_out, zero_out, one_out, two_out):
@@ -525,6 +560,10 @@
         n = dims[part][stage]
         inner = dims[part][stage + 1 :]
         return pltpu.VMEM((2 * (n - 1), inner[0] // 2, *inner[1:], *tile[part]), F32)
+
+    def leaf(part):
+        pairs = dims[part][1] // 2 * dims[part][2] * TILES_OF[part] // 2
+        return pltpu.VMEM((4, pairs, 16, LANES), BF16)
 
     dma = pltpu.SemaphoreType.DMA
     nodes, tiles = pl.pallas_call(
@@ -553,12 +592,14 @@
             *[ring(p, 1) for p in range(3)],
             *[pltpu.VMEM((dims[p][2], *tile[p]), F32) for p in range(3)],
             *[pltpu.VMEM((dims[p][2] - 1, *tile[p]), F32) for p in range(3)],
+            *[leaf(p) for p in range(3)],
+            *[leaf(p) for p in range(3)],
             pltpu.VMEM((8, 12, 8, LANES), F32),
             pltpu.VMEM((NZ, 120, 2 * LANES), F32),
             pltpu.VMEM((2, 8, width), F32),
             dma((3,)), dma((5,)), dma((5,)),
             dma((3, 14)), dma((3, 14)), dma((3, 14)), dma((3, 14)), dma((3, 7)), dma((3, 7)),
-            dma((3, 7)), dma((3, 7)), dma((2,)), dma((2,)), dma((2,)), dma((2,)),
+            dma((3, 7)), dma((3, 7)), dma((2,)), dma((2,)), dma((3, 2)), dma((3, 2)),
         ],
         compiler_params=pltpu.CompilerParams(
             vmem_limit_bytes=VMEM_LIMIT, collective_id=0, has_side_effects=True

time: 83 us -> 73.6 us (0.89)
  Pallas kernels: 82.3 us -> 72.6 us
    pallas_call x1, Pallas kernels: 80.5 us -> 70.8 us  [shards(): pl.pallas_call(edge_kernel, out_shape=(jax.ShapeDtypeStruct((16, width),...]
where the time goes in v3:
time: 73.6 us; the launch traced here: 73.3 us
  Pallas kernels  72.6 us (99%)
    pallas_call x1, Pallas kernels, shards(): pl.pallas_call(edge_kernel, out_shape=(jax.ShapeDtypeStruct((16, width),...  70.8 us
    pallas_call x1, Pallas kernels, shards(): pl.pallas_call(place_kernel, out_shape=(jax.ShapeDtypeStruct((16, width),...  1.8 us

profile of v3, /device:TPU:1, one launch (start us, length us, event | category | flops | bytes accessed | tf_op | source)
XLA Modules:
  0.0 73.3 jit_solution(5736565833069743648)
XLA Ops:
  0.6 70.8 %edge_gradients.1 = (bf16[16,3712]{1,0:T(8,128)(2,1)}, f32[8,12,8,128]{3,2,1,0:T(8,128)}) custom-call(bf16[16,3712]{1,0:T(8,128)(2,1)} %bitcast.3, bf16[16,3712]{1,0:T(8,128)(2,1)} %bitcast.4, s32[1,320]{1,0:T(1,128)} %source_ref.1, s32[1,320]{1,0:T(1,128)} %target_ref.1, f32[1,320]{1,0:T(1,128)} %angle_ref.1, bf16[896,896]{1,0:T(8,128)(2,1)} %w0_hbm.1, ...), custom_call_target="tpu_custom_call" | custom-call | tf_op jit(solution)/shard_map/edge_gradients/pallas_call | solution.py:569
  71.5 1.8 %place_tiles.1 = (bf16[16,3712]{1,0:T(8,128)(2,1)}, f32[28,896]{1,0:T(8,128)}, f32[24,1536]{1,0:T(8,128)}, f32[20,1280]{1,0:T(8,128)}) custom-call(f32[8,12,8,128]{3,2,1,0:T(8,128)} %get-tuple-element.10.tiles_ref, bf16[16,3712]{1,0:T(8,128)(2,1)} %get-tuple-element.11.nodes_ref), custom_call_target="tpu_custom_call" | custom-call | tf_op jit(solution)/shard_map/place_tiles/pallas_call | solution.py:609

commit v4 on v3

--- a/solution.py
+++ b/solution.py
@@ -64,8 +64,14 @@
 
 
 SHARES = (
-    ((0, 7, 29), (1, 7, 21), (1, 24, 26)),
+    (
+        (0, 7, 29), (1, 7, 9), (1, 13, 15), (1, 9, 11), (1, 15, 17), (1, 11, 13), (1, 17, 19),
+        (1, 19, 21), (1, 24, 26),
+    ),
     ((0, 0, 7), (0, 19, 29), (1, 0, 7), (1, 21, 24), (1, 26, 29)),
+)
+MADE = (
+    7, 8, 13, 14, 0, 1, 2, 3, 4, 5, 6, 9, 10, 15, 16, 11, 12, 17, 18, 19, 20, 24, 25, 21, 22, 23, 26, 27, 28,
 )
 ONE_ORDER = tuple(b for j in range(3) for b in (2 * j, 2 * j + 1, 6 + 2 * j, 7 + 2 * j))
 TILES = (
@@ -181,10 +187,11 @@
             src = ring[part].at[slot - 1]
         return remote(src, ring[part].at[slot], sends.at[part, slot], recvs.at[part, slot], moved(axis, way))
 
-    def begin(part, stage):
+    def begin(part, stage, picked=(0, 1, 2, 3)):
         axis = AXES[part][stage]
         n = COUNT[axis]
-        for chain, (way, half, steps) in enumerate(chains_of(n)):
+        for chain in picked:
+            way, half, steps = chains_of(n)[chain]
             if stage == 0:
                 deep = stage1[part].shape[1] // 2
                 block = (place[axis] + way * steps + n) % n
@@ -199,13 +206,13 @@
             return ins16[part][chain].astype(F32).reshape(ring.shape[1:])
         return ring[slot_of(n, chain, step)]
 
-    def advance(part, stage, step):
+    def advance(part, stage, step, picked=(0, 1, 2, 3)):
         axis = AXES[part][stage]
         n = COUNT[axis]
         source, ring = ((stage1, rings1), (stage2, rings2))[stage]
         deep = source[part].shape[1] // 2
         for chain, (way, half, steps) in enumerate(chains_of(n)):
-            if step < steps:
+            if step < steps and chain in picked:
                 slot = slot_of(n, chain, step)
                 ring_copy(part, stage, chain, step - 1).wait_recv()
                 block = (place[axis] + way * (steps - step) + n) % n
@@ -262,7 +269,7 @@
     def ready(had, have):
         for part in range(3):
             if had < 4 * (FIRST_OF[part] + TILES_OF[part]) <= have:
-                begin(part, 0)
+                begin(part, 0, (0, 1))
 
     def put(which, tile, row_y, v):
         at = PLACE[which][tile]
@@ -376,15 +383,16 @@
             keep_x(minus + at, width, n.astype(BF16))
 
 
-    def share(kind, lo, hi):
+    def share(chosen):
         for other in range(2):
-            @pl.when(core == 1 - other)
-            def _(other=other):
-                for k, span in enumerate(SHARES[other]):
-                    if span[0] == kind and lo < span[2] <= hi:
-                        share_copy(k, span).start()
-
-    share(0, 0, BLOCKS)
+            spans = [k for k, span in enumerate(SHARES[other]) if chosen(*span)]
+            if spans:
+                @pl.when(core == 1 - other)
+                def _(other=other, spans=spans):
+                    for k in spans:
+                        share_copy(k, SHARES[other][k]).start()
+
+    share(lambda kind, lo, hi: kind == 0)
     for load in loads:
         load.wait()
     total = jnp.zeros((EDGES, LANES), F32)
@@ -420,13 +428,12 @@
     scale = 1.0 / (float(size) ** 0.5)
     gate = jax.nn.sigmoid(head_sum(first) * scale)
     dlogit = head_sum(total) * gate * (1.0 - gate) * scale
-    for block in range(BLOCKS):
+    for block in MADE:
         v = du_s[:, cols(block)] * gate
         if block == 0:
             v = v + dlogit
         d_s[block, :EDGES, :] = v.astype(BF16)
-        if any(block + 1 == span[2] for spans in SHARES for span in spans if span[0]):
-            share(1, block, block + 1)
+        share(lambda kind, lo, hi: kind == 1 and block + 1 == hi)
 
 
     atoms = node_ref.shape[0]
@@ -458,14 +465,17 @@
         scatter(at, width, dot_t(dz, w0_ref[cols(at, width), :]))
     @pl.when(core == 0)
     def _():
-        for k, span in enumerate(SHARES[0]):
-            share_copy(k, span).wait_recv()
+        share_copy(0, SHARES[0][0]).wait_recv()
         for j in range(3):
+            for k in (1 + 2 * j, 2 + 2 * j):
+                share_copy(k, SHARES[0][k]).wait_recv()
             dp_, dn_ = pair(AT_P1 + 2 * j, 2), pair(AT_N1 + 2 * j, 2)
             rp, rn = factor(AT_P1, ONE), factor(AT_N1, ONE)
             put_aligned(dot(rp, dp_) + dot(rn, dn_), (2 * j, 2 * j + 1))
             put_aligned(dot(rp, dn_) - dot(rn, dp_), (6 + 2 * j, 7 + 2 * j))
             ready(12 * j, 12 * j + 12)
+        for k in (7, 8):
+            share_copy(k, SHARES[0][k]).wait_recv()
         two_blocks(0, 0, 2)
         ready(36, 48)
         for k, span in enumerate(SHARES[1]):
@@ -473,8 +483,8 @@
 
     @pl.when(core == 1)
     def _():
-        for k, span in enumerate(SHARES[1]):
-            share_copy(k, span).wait_recv()
+        for k in (0, 2):
+            share_copy(k, SHARES[1][k]).wait_recv()
         blank = jnp.zeros((NZ, 8, LANES), F32)
         for row_y in range(NY):
             for at in (46, 47):
@@ -482,45 +492,54 @@
         for at, width in chunks(ZERO):
             put_shifted(1, 0, 4, 28, dot(factor(AT_Z, ZERO), pair(AT_Z + at, width)), range(at, at + width))
             ready(4 * at, 4 * (at + width))
+        for k in (1, 3, 4):
+            share_copy(k, SHARES[1][k]).wait_recv()
         two_blocks(1, 2, 2)
         two_blocks(1, 4, 1)
         ready(28, 48)
         for k, span in enumerate(SHARES[0]):
             share_copy(k, span).wait_send()
 
+    begin(0, 0, (2, 3))
+    advance(0, 0, 1, (0, 1))
+    begin(1, 0, (2, 3))
+    begin(2, 0, (2, 3))
+    advance(0, 0, 1, (2, 3))
     back(0, slice(0, 1))
-    advance(0, 0, 1)
-    back(0, slice(1, 3))
-    advance(0, 0, 2)
     advance(1, 0, 1)
     advance(2, 0, 1)
+    advance(0, 0, 2, (0, 1))
+    advance(0, 0, 2, (2, 3))
+    back(0, slice(1, 2))
+    advance(0, 0, 3)
+    back(0, slice(2, 3))
+    finish(1, 0, s21)
+    begin(1, 1)
+    finish(0, 0, s20)
+    begin(0, 1)
+    finish(2, 0, s22)
+    begin(2, 1)
     back(1, slice(0, 1))
-    advance(0, 0, 3)
-    back(1, slice(1, 3))
+    advance(1, 1, 1)
+    advance(0, 1, 1)
+    advance(2, 1, 1)
+    back(1, slice(1, 2))
+    finish(1, 1, s31)
+    last_begin(1)
+    finish(0, 1, s30)
+    last_begin(0)
+    finish(2, 1, s32)
+    last_begin(2)
+    back(1, slice(2, 3))
     node_up.start()
     node_down.start()
-    finish(0, 0, s20)
-    begin(0, 1)
-    finish(1, 0, s21)
-    begin(1, 1)
-    finish(2, 0, s22)
-    begin(2, 1)
-    advance(0, 1, 1)
-    advance(1, 1, 1)
-    advance(2, 1, 1)
-    finish(0, 1, s30)
-    last_begin(0)
-    finish(1, 1, s31)
-    last_begin(1)
-    finish(2, 1, s32)
-    last_begin(2)
     last_end(0)
+    last_end(1)
+    last_end(2)
     node_up.wait()
     node_down.wait()
     nodes_out[pl.ds(0, 8)] = (node_ref[pl.ds(8, 8)] + node_in[0]).astype(BF16)
     nodes_out[pl.ds(8, 8)] = (node_ref[pl.ds(16, 8)] + node_in[1]).astype(BF16)
-    last_end(1)
-    last_end(2)
     for part in range(3):
         for stage in range(2):
             sent(part, stage)
@@ -597,7 +616,7 @@
             pltpu.VMEM((8, 12, 8, LANES), F32),
             pltpu.VMEM((NZ, 120, 2 * LANES), F32),
             pltpu.VMEM((2, 8, width), F32),
-            dma((3,)), dma((5,)), dma((5,)),
+            dma((3,)), dma((9,)), dma((9,)),
             dma((3, 14)), dma((3, 14)), dma((3, 14)), dma((3, 14)), dma((3, 7)), dma((3, 7)),
             dma((3, 7)), dma((3, 7)), dma((2,)), dma((2,)), dma((3, 2)), dma((3, 2)),
         ],

time: 73.6 us -> 70.8 us (0.962)
  Pallas kernels: 72.6 us -> 70.1 us
    pallas_call x1, Pallas kernels: 70.8 us -> 68.3 us  [shards(): pl.pallas_call(edge_kernel, out_shape=(jax.ShapeDtypeStruct((16, width),...]
where the time goes in v4:
time: 70.8 us; the launch traced here: 70.7 us
  Pallas kernels  70.1 us (99%)
    pallas_call x1, Pallas kernels, shards(): pl.pallas_call(edge_kernel, out_shape=(jax.ShapeDtypeStruct((16, width),...  68.3 us
    pallas_call x1, Pallas kernels, shards(): pl.pallas_call(place_kernel, out_shape=(jax.ShapeDtypeStruct((16, width),...  1.8 us

profile of v4, /device:TPU:1, one launch (start us, length us, event | category | flops | bytes accessed | tf_op | source)
XLA Modules:
  0.0 70.7 jit_solution(8082864379850310148)
XLA Ops:
  0.6 68.3 %edge_gradients.1 = (bf16[16,3712]{1,0:T(8,128)(2,1)}, f32[8,12,8,128]{3,2,1,0:T(8,128)}) custom-call(bf16[16,3712]{1,0:T(8,128)(2,1)} %bitcast.3, bf16[16,3712]{1,0:T(8,128)(2,1)} %bitcast.4, s32[1,320]{1,0:T(1,128)} %source_ref.1, s32[1,320]{1,0:T(1,128)} %target_ref.1, f32[1,320]{1,0:T(1,128)} %angle_ref.1, bf16[896,896]{1,0:T(8,128)(2,1)} %w0_hbm.1, ...), custom_call_target="tpu_custom_call" | custom-call | tf_op jit(solution)/shard_map/edge_gradients/pallas_call | solution.py:588
  68.9 1.8 %place_tiles.1 = (bf16[16,3712]{1,0:T(8,128)(2,1)}, f32[28,896]{1,0:T(8,128)}, f32[24,1536]{1,0:T(8,128)}, f32[20,1280]{1,0:T(8,128)}) custom-call(f32[8,12,8,128]{3,2,1,0:T(8,128)} %get-tuple-element.10.tiles_ref, bf16[16,3712]{1,0:T(8,128)(2,1)} %get-tuple-element.11.nodes_ref), custom_call_target="tpu_custom_call" | custom-call | tf_op jit(solution)/shard_map/place_tiles/pallas_call | solution.py:628

commit v5 on v4

--- a/solution.py
+++ b/solution.py
@@ -460,9 +460,11 @@
             scatter(minus + at, width, c * back_n - s * back_p)
 
 
-    dz = dconv(AT_Z, ZERO)
-    for at, width in chunks(ZERO):
-        scatter(at, width, dot_t(dz, w0_ref[cols(at, width), :]))
+    def back_zero(picked):
+        dz = dconv(AT_Z, ZERO)
+        for at, width in chunks(ZERO)[picked]:
+            scatter(at, width, dot_t(dz, w0_ref[cols(at, width), :]))
+
     @pl.when(core == 0)
     def _():
         share_copy(0, SHARES[0][0]).wait_recv()
@@ -505,21 +507,21 @@
     begin(1, 0, (2, 3))
     begin(2, 0, (2, 3))
     advance(0, 0, 1, (2, 3))
-    back(0, slice(0, 1))
+    back_zero(slice(0, 4))
     advance(1, 0, 1)
     advance(2, 0, 1)
     advance(0, 0, 2, (0, 1))
     advance(0, 0, 2, (2, 3))
+    back(0, slice(0, 1))
+    advance(0, 0, 3)
     back(0, slice(1, 2))
-    advance(0, 0, 3)
-    back(0, slice(2, 3))
     finish(1, 0, s21)
     begin(1, 1)
     finish(0, 0, s20)
     begin(0, 1)
     finish(2, 0, s22)
     begin(2, 1)
-    back(1, slice(0, 1))
+    back(0, slice(2, 3))
     advance(1, 1, 1)
     advance(0, 1, 1)
     advance(2, 1, 1)
@@ -528,6 +530,7 @@
     last_begin(1)
     finish(0, 1, s30)
     last_begin(0)
+    back(1, slice(0, 1))
     finish(2, 1, s32)
     last_begin(2)
     back(1, slice(2, 3))

time: 70.8 us -> 70.4 us (level)
  no operation moved by 1% of the time
where the time goes in v5:
time: 70.4 us; the launch traced here: 70.3 us
  Pallas kernels  69.7 us (99%)
    pallas_call x1, Pallas kernels, shards(): pl.pallas_call(edge_kernel, out_shape=(jax.ShapeDtypeStruct((16, width),...  67.9 us
    pallas_call x1, Pallas kernels, shards(): pl.pallas_call(place_kernel, out_shape=(jax.ShapeDtypeStruct((16, width),...  1.8 us

profile of v5, /device:TPU:1, one launch (start us, length us, event | category | flops | bytes accessed | tf_op | source)
XLA Modules:
  0.0 70.3 jit_solution(2512210503067611055)
XLA Ops:
  0.6 67.9 %edge_gradients.1 = (bf16[16,3712]{1,0:T(8,128)(2,1)}, f32[8,12,8,128]{3,2,1,0:T(8,128)}) custom-call(bf16[16,3712]{1,0:T(8,128)(2,1)} %bitcast.3, bf16[16,3712]{1,0:T(8,128)(2,1)} %bitcast.4, s32[1,320]{1,0:T(1,128)} %source_ref.1, s32[1,320]{1,0:T(1,128)} %target_ref.1, f32[1,320]{1,0:T(1,128)} %angle_ref.1, bf16[896,896]{1,0:T(8,128)(2,1)} %w0_hbm.1, ...), custom_call_target="tpu_custom_call" | custom-call | tf_op jit(solution)/shard_map/edge_gradients/pallas_call | solution.py:591
  68.5 1.8 %place_tiles.1 = (bf16[16,3712]{1,0:T(8,128)(2,1)}, f32[28,896]{1,0:T(8,128)}, f32[24,1536]{1,0:T(8,128)}, f32[20,1280]{1,0:T(8,128)}) custom-call(f32[8,12,8,128]{3,2,1,0:T(8,128)} %get-tuple-element.10.tiles_ref, bf16[16,3712]{1,0:T(8,128)(2,1)} %get-tuple-element.11.nodes_ref), custom_call_target="tpu_custom_call" | custom-call | tf_op jit(solution)/shard_map/place_tiles/pallas_call | solution.py:631

commit v6 on v5

--- a/solution.py
+++ b/solution.py
@@ -97,9 +97,9 @@
 
 
 def edge_kernel(
-    feats_ref, cotan_ref, source_ref, target_ref, angle_ref, w0_hbm, w1_hbm, w2_hbm,
+    feats_hbm, cotan_hbm, source_hbm, target_hbm, angle_hbm, w0_hbm, w1_hbm, w2_hbm,
     nodes_out, tiles_out,
-    w0_ref, w1_ref, w2_ref, tab_ref, x_s, du_s, trig_s, oh_s, node_ref,
+    feats_ref, cotan_ref, source_ref, target_ref, angle_ref, w0_ref, w1_ref, w2_ref, tab_ref, x_s, du_s, trig_s, oh_s, node_ref,
     xt_s, d_s, part0, part1, part2, r10, r11, r12, s20, s21, s22, r20, r21, r22, s30, s31, s32, r30, r31, r32,
     o0, o1, o2, i0, i1, i2, gathered, result, node_in,
     load_sem, share_send, share_recv, send1, recv1, send2, recv2, send3, recv3, all_send, all_recv, node_send, node_recv,
@@ -127,15 +127,18 @@
     peers = [{"dp": (dp + o) % 8, "graph": graph} for o in range(1, 8)]
     peers += [moved("y", o) for o in range(1, NY)] + [moved("z", o) for o in range(1, NZ)] + [before, after]
 
+    inputs = (
+        (feats_hbm, feats_ref), (cotan_hbm, cotan_ref), (source_hbm, source_ref), (target_hbm, target_ref),
+        (angle_hbm, angle_ref), (w0_hbm, w0_ref), (w1_hbm, w1_ref), (w2_hbm, w2_ref),
+    )
+    loads = [pltpu.make_async_copy(src, dst, load_sem.at[k]) for k, (src, dst) in enumerate(inputs)]
+    for load in loads:
+        load.start()
     barrier = pltpu.get_barrier_semaphore()
     for peer in peers:
         pl.semaphore_signal(barrier, inc=1, device_id=peer, device_id_type=MESH)
-    loads = [
-        pltpu.make_async_copy(src, dst, load_sem.at[k])
-        for k, (src, dst) in enumerate(((w0_hbm, w0_ref), (w1_hbm, w1_ref), (w2_hbm, w2_ref)))
-    ]
-    for load in loads:
-        load.start()
+    for load in loads[:5]:
+        load.wait()
     feats, cotan = feats_ref[...].astype(F32), cotan_ref[...].astype(F32)
     tab_ref[pl.ds(0, 16)] = jnp.concatenate([feats[:8], cotan[:8]], 0).astype(BF16)
     tab_ref[pl.ds(16, 16)] = jnp.concatenate([feats[8:], cotan[8:]], 0).astype(BF16)
@@ -393,7 +396,7 @@
                         share_copy(k, SHARES[other][k]).start()
 
     share(lambda kind, lo, hi: kind == 0)
-    for load in loads:
+    for load in loads[5:]:
         load.wait()
     total = jnp.zeros((EDGES, LANES), F32)
     first = None
@@ -594,9 +597,14 @@
             jax.ShapeDtypeStruct((16, width), BF16),
             jax.ShapeDtypeStruct((8, 12, 8, LANES), F32),
         ),
-        in_specs=[vmem] * 5 + [hbm] * 3,
+        in_specs=[hbm] * 8,
         out_specs=(vmem,) * 2,
         scratch_shapes=[
+            pltpu.VMEM(node_feats.shape[1:], BF16),
+            pltpu.VMEM(node_cotan.shape[1:], BF16),
+            pltpu.VMEM(source.shape, jnp.int32),
+            pltpu.VMEM(target.shape, jnp.int32),
+            pltpu.VMEM(angle.shape, F32),
             pltpu.VMEM(w_zero.shape, BF16),
             pltpu.VMEM(w_one.shape, BF16),
             pltpu.VMEM(w_two.shape, BF16),
@@ -619,7 +627,7 @@
             pltpu.VMEM((8, 12, 8, LANES), F32),
             pltpu.VMEM((NZ, 120, 2 * LANES), F32),
             pltpu.VMEM((2, 8, width), F32),
-            dma((3,)), dma((9,)), dma((9,)),
+            dma((8,)), dma((9,)), dma((9,)),
             dma((3, 14)), dma((3, 14)), dma((3, 14)), dma((3, 14)), dma((3, 7)), dma((3, 7)),
             dma((3, 7)), dma((3, 7)), dma((2,)), dma((2,)), dma((3, 2)), dma((3, 2)),
         ],

time: 70.4 us -> 69.8 us (level)
  no operation moved by 1% of the time
where the time goes in v6:
time: 69.8 us; the launch traced here: 69.7 us
  Pallas kernels  69.1 us (99%)
    pallas_call x1, Pallas kernels, shards(): pl.pallas_call(edge_kernel, out_shape=(jax.ShapeDtypeStruct((16, width),...  67.2 us
    pallas_call x1, Pallas kernels, shards(): pl.pallas_call(place_kernel, out_shape=(jax.ShapeDtypeStruct((16, width),...  1.8 us

profile of v6, /device:TPU:1, one launch (start us, length us, event | category | flops | bytes accessed | tf_op | source)
XLA Modules:
  0.0 69.7 jit_solution(3232553103238047316)
XLA Ops:
  0.6 67.2 %edge_gradients.1 = (bf16[16,3712]{1,0:T(8,128)(2,1)}, f32[8,12,8,128]{3,2,1,0:T(8,128)}) custom-call(bf16[16,3712]{1,0:T(8,128)(2,1)} %bitcast.3, bf16[16,3712]{1,0:T(8,128)(2,1)} %bitcast.4, s32[1,320]{1,0:T(1,128)} %source_hbm.1, s32[1,320]{1,0:T(1,128)} %target_hbm.1, f32[1,320]{1,0:T(1,128)} %angle_hbm.1, bf16[896,896]{1,0:T(8,128)(2,1)} %w0_hbm.1, ...), custom_call_target="tpu_custom_call" | custom-call | tf_op jit(solution)/shard_map/edge_gradients/pallas_call | solution.py:594
  67.9 1.8 %place_tiles.1 = (bf16[16,3712]{1,0:T(8,128)(2,1)}, f32[28,896]{1,0:T(8,128)}, f32[24,1536]{1,0:T(8,128)}, f32[20,1280]{1,0:T(8,128)}) custom-call(f32[8,12,8,128]{3,2,1,0:T(8,128)} %get-tuple-element.10.tiles_ref, bf16[16,3712]{1,0:T(8,128)(2,1)} %get-tuple-element.11.nodes_ref), custom_call_target="tpu_custom_call" | custom-call | tf_op jit(solution)/shard_map/place_tiles/pallas_call | solution.py:639
